TPU v7x, 768 devices: a whole 4x8x12 slice. The times are simulated.
768 devices in a mesh: dp: 24 (over z, core), seq: 32 (over y, x).
Axes of the slice: x: 4, y: 8, z: 12, core: 2. Of those that a mesh axis runs over, the one named last changes fastest.
Arguments:
- enc: bfloat16 [98304, 2048], P(('dp', 'seq')), may hold values from -6 to 6
- enc_dest: int32 [98304, 1], P(('dp', 'seq')), may hold values from 0 to 31; in each aligned block of 128 rows (0 to 127, 128 to 255, ...) at most 6 rows name the same one
- enc_group: int32 [98304], P(('dp', 'seq')), may hold values from 0 to 7
- query: bfloat16 [196608, 1024], P(('dp', 'seq')), may hold values from -12 to 12
- dec_group: int32 [196608], P(('dp', 'seq')), may hold values from 0 to 7
- out_grad: bfloat16 [196608, 1024], P(('dp', 'seq')), may hold values from -6 to 6
- w_kv: bfloat16 [2048, 2048], replicated, may hold values from -0.125 to 0.125
Outputs:
- query_grad: bfloat16 [196608, 1024], P(('dp', 'seq'))
- enc_grad: bfloat16 [98304, 2048], P(('dp', 'seq'))
- kv_weight_grad: float32 [2048, 2048], P('seq')
Inputs may be any that keep to these rules, and one draw needn't show every extreme that they name: `enc_dest`: of the 128 encoder tokens of one device, at most 6 name any one decoder owner, and in every draw some owner is named by exactly 6 of them.
All inputs are finite; a program needn't handle non-finite values.
Results may differ from a plain program's by a relative error of at most 0.02.
Values may be sent and summed in bfloat16 or wider, within the bound.
No kernel may reach another device: no remote copies, remote signals or barrier semaphores. Data moves between devices by JAX's collectives and lax.ppermute only.
A program may use at most 64 MiB of HBM per device.

v0:
```python
import math

import jax
import jax.numpy as jnp
from jax import lax
from jax.sharding import PartitionSpec as P

HEADS = 8
HEAD_DIM = 128


def shards(enc, enc_dest, enc_group, query, dec_group, out_grad, w_kv):
    peers = lax.axis_size("seq")
    enc_rows = enc.shape[0]
    capacity = 3 * enc_rows // (2 * peers)
    slot_count = peers * capacity
    width = w_kv.shape[1] // 2
    dec_rows = query.shape[0]
    scale = 1.0 / math.sqrt(HEAD_DIM)
    norm_factor = 1.0 / math.sqrt(enc_rows * peers * lax.axis_size("dp"))
    dest = enc_dest[:, 0]
    hits = (dest[:, None] == jnp.arange(peers, dtype=jnp.int32)[None, :]).astype(jnp.int32)
    before = jnp.cumsum(hits, axis=0) - hits
    rank = jnp.sum(before * hits, axis=1)
    target = dest * capacity + rank
    placing = (target[:, None] == jnp.arange(slot_count, dtype=jnp.int32)[None, :]).astype(
        jnp.bfloat16
    )

    def spread(rows):
        return lax.dot_general(
            placing, rows, (((0,), (0,)), ((), ())), preferred_element_type=jnp.float32
        ).astype(jnp.bfloat16)

    label_out = spread((enc_group + 1).astype(jnp.bfloat16)[:, None]).reshape(peers, capacity)
    sent, label_in = (
        lax.all_to_all(
            spread(enc).reshape(peers, capacity, -1), "seq", split_axis=0, concat_axis=0, tiled=True
        ),
        lax.all_to_all(label_out, "seq", split_axis=0, concat_axis=0, tiled=True),
    )
    slot_kv = jnp.dot(
        sent.reshape(slot_count, -1), w_kv, preferred_element_type=jnp.float32
    ).astype(jnp.bfloat16)
    labels = label_in.reshape(slot_count).astype(jnp.float32)
    allowed = (labels[None, :] == (dec_group + 1).astype(jnp.float32)[:, None])[None]
    queries = query.reshape(dec_rows, HEADS, HEAD_DIM)
    grads_in = out_grad.reshape(dec_rows, HEADS, HEAD_DIM)
    keys = slot_kv[:, :width].reshape(slot_count, HEADS, HEAD_DIM)
    values = slot_kv[:, width:].reshape(slot_count, HEADS, HEAD_DIM)
    score = jnp.einsum("thd,rhd->htr", queries, keys, preferred_element_type=jnp.float32) * scale
    top = jnp.maximum(jnp.max(jnp.where(allowed, score, 0.0), axis=-1, keepdims=True), 0.0)
    expo = jnp.where(allowed, jnp.exp(score - top), 0.0)
    weight = expo / (jnp.exp(-top) + jnp.sum(expo, axis=-1, keepdims=True))
    probs = weight.astype(jnp.bfloat16)
    attended = jnp.einsum("htr,rhd->thd", probs, values, preferred_element_type=jnp.float32)
    delta = jnp.sum(grads_in.astype(jnp.float32) * attended, axis=2).T
    value_dot = jnp.einsum("thd,rhd->htr", grads_in, values, preferred_element_type=jnp.float32)
    score_grad = (weight * (value_dot - delta[:, :, None]) * scale).astype(jnp.bfloat16)
    query_grad = (
        jnp.einsum("htr,rhd->thd", score_grad, keys, preferred_element_type=jnp.float32)
        .reshape(dec_rows, width)
        .astype(jnp.bfloat16)
    )
    key_grad = jnp.einsum(
        "htr,thd->rhd", score_grad, queries, preferred_element_type=jnp.float32
    ).reshape(slot_count, width)
    value_grad = jnp.einsum(
        "htr,thd->rhd", probs, grads_in, preferred_element_type=jnp.float32
    ).reshape(slot_count, width)
    slot_grad = jnp.concatenate([key_grad, value_grad], axis=1).astype(jnp.bfloat16)
    returned = lax.all_to_all(
        slot_grad.reshape(peers, capacity, -1), "seq", split_axis=0, concat_axis=0, tiled=True
    )
    kv_grad = jnp.dot(
        placing, returned.reshape(slot_count, -1), preferred_element_type=jnp.float32
    ).astype(jnp.bfloat16)
    enc_grad = lax.dot_general(
        kv_grad, w_kv, (((1,), (1,)), ((), ())), preferred_element_type=jnp.float32
    ).astype(jnp.bfloat16)
    partial_value = (
        lax.dot_general(enc, kv_grad, (((0,), (0,)), ((), ())), preferred_element_type=jnp.float32)
        * norm_factor
    )
    shares = lax.psum_scatter(
        partial_value.astype(jnp.bfloat16), "seq", scatter_dimension=0, tiled=True
    ).astype(jnp.float32)
    kv_weight_grad = lax.psum(shares, "dp")
    return (query_grad, enc_grad, kv_weight_grad)


def solution(mesh):
    in_specs = (
        P(("dp", "seq"), None),
        P(("dp", "seq"), None),
        P(("dp", "seq")),
        P(("dp", "seq"), None),
        P(("dp", "seq")),
        P(("dp", "seq"), None),
        P(),
    )
    out_specs = (P(("dp", "seq"), None), P(("dp", "seq"), None), P("seq", None))
    return jax.shard_map(shards, mesh=mesh, in_specs=in_specs, out_specs=out_specs, check_vma=False)
```

profile of v0, /device:TPU:1, one launch (start us, length us, event | category | flops | bytes accessed | tf_op | source)
XLA Modules:
  0.0 453.0 jit_solution(8526780073975967369)
XLA Ops:
  7.2 0.8 fusion.30
  8.2 0.8 select_reduce_fusion
  9.0 0.7 fusion.32
  9.7 0.9 fusion.26
  10.5 0.7 all_to_all.16
  11.2 10.5 %all-to-all-start.1 = ((bf16[32,1,6]{2,1,0:T(2,128)(2,1)}), bf16[32,1,6]{2,1,0:T(2,128)(2,1)S(1)}, u32[]{:S(2)}, u32[]{:S(2)}) async-start(bf16[32,1,6]{2,1,0:T(2,128)(2,1)} %all_to_all.16), calls=%async_computation.1 | async-start | bytes 32768 | tf_op jit(solution)/shard_map/all_to_all | solution.py:40
  22.3 1.2 reshape.98
  23.5 6.8 %all-to-all-done.1 = bf16[32,1,6]{2,1,0:T(2,128)(2,1)S(1)} async-done(((bf16[32,1,6]{2,1,0:T(2,128)(2,1)}), bf16[32,1,6]{2,1,0:T(2,128)(2,1)S(1)}, u32[]{:S(2)}, u32[]{:S(2)}) %all-to-all-start.1) | async-done | bytes 416 | tf_op jit(solution)/shard_map/all_to_all | solution.py:40
  30.3 3.9 all-to-all-start
  34.3 1.0 copy.37
  35.5 20.9 %all-to-all-done = bf16[32,6,2048]{2,1,0:T(8,128)(2,1)S(1)} async-done(((bf16[32,6,2048]{2,1,0:T(8,128)(2,1)}), bf16[32,6,2048]{2,1,0:T(8,128)(2,1)S(1)}, u32[]{:S(2)}, u32[]{:S(2)}) %all-to-all-start) | async-done | bytes 786464 | tf_op jit(solution)/shard_map/all_to_all | solution.py:37
  56.7 5.2 %convolution_convert_fusion = bf16[192,2048]{1,0:T(8,128)(2,1)S(1)} fusion(bf16[192,2048]{1,0:T(8,128)(2,1)S(1)} %reshape.99, bf16[2048,2048]{1,0:T(8,128)(2,1)} %param.13), kind=kOutput, calls=%fused_computation.2 | convolution fusion | flops 1611005952 | bytes 9961472 | tf_op jit(solution)/shard_map/dot_general | solution.py:42
  61.9 1.0 copy-done.2
  64.4 0.6 fusion.9
  65.0 0.6 fusion.2
  67.7 29.1 %all_to_all.20 = bf16[32,6,2048]{2,1,0:T(8,128)(2,1)S(1)} all-to-all(bf16[32,6,2048]{2,1,0:T(8,128)(2,1)S(1)} %pad_maximum_fusion), channel_id=1, replica_groups=mesh['dp'=24,'seq'=32] {'seq'}, dimensions={0} | all-to-all | bytes 1572864 | tf_op jit(solution)/shard_map/all_to_all | solution.py:72
  97.4 5.6 %fusion = bf16[2048,2048]{0,1:T(8,128)(2,1)} fusion(bf16[128,2048]{1,0:T(8,128)(2,1)S(1)} %convolution_convert_fusion.3, bf16[128,2048]{1,0:T(8,128)(2,1)S(1)} %copy-done), kind=kOutput, calls=%fused_computation.1 | convolution fusion | flops 1082130432 | bytes 9437184 | tf_op jit(solution)/shard_map/dot_general | solution.py:82
  103.0 12.3 %copy.50 = bf16[2048,2048]{1,0:T(8,128)(2,1)} copy(bf16[2048,2048]{0,1:T(8,128)(2,1)} %fusion) | data formatting | bytes 16777216
  115.7 1.0 copy.46
  116.7 7.1 %convolution_convert_fusion.2 = bf16[128,2048]{1,0:T(8,128)(2,1)} fusion(bf16[128,2048]{1,0:T(8,128)(2,1)S(1)} %convolution_convert_fusion.3, bf16[2048,2048]{1,0:T(8,128)(2,1)} %param.13), kind=kOutput, calls=%fused_computation.4 | convolution fusion | flops 1074003968 | bytes 9437184 | tf_op jit(solution)/shard_map/dot_general | solution.py:78
  123.8 238.2 %reduce-scatter.4.cloned.1.call-done = bf16[64,2048]{1,0:T(8,128)(2,1)} async-done(((bf16[2048,2048]{1,0:T(8,128)(2,1)}), bf16[64,2048]{1,0:T(8,128)(2,1)}) %reduce-scatter.4.cloned.1.call-update) | async-done | bytes 262160
  362.0 1.2 copy.51
  363.2 81.8 %all-reduce.1 = f32[64,2048]{0,1:T(8,128)S(1)} all-reduce(bf16[64,2048]{0,1:T(8,128)(2,1)S(1)} %copy.51), channel_id=1, replica_groups=mesh['dp'=24,'seq'=32] {'dp'}, use_global_device_ids=true, to_apply=%region_6.7 | all-reduce | flops 131072 | bytes 786432 | tf_op jit(solution)/shard_map/psum | solution.py:88
  445.1 1.1 copy.47
  (34 shorter events, 5.7 us)
Async XLA Ops:
  7.2 14.6 %copy-start = (bf16[128,2048]{1,0:T(8,128)(2,1)S(1)}, bf16[128,2048]{1,0:T(8,128)(2,1)}, u32[]{:S(2)}) copy-start(bf16[128,2048]{1,0:T(8,128)(2,1)} %param.7) | copy-start | bytes 1572868
  11.2 19.0 %all-to-all-start.1 = ((bf16[32,1,6]{2,1,0:T(2,128)(2,1)}), bf16[32,1,6]{2,1,0:T(2,128)(2,1)S(1)}, u32[]{:S(2)}, u32[]{:S(2)}) async-start(bf16[32,1,6]{2,1,0:T(2,128)(2,1)} %all_to_all.16), calls=%async_computation.1 | async-start | bytes 32768 | tf_op jit(solution)/shard_map/all_to_all | solution.py:40
  22.2 12.0 %copy-start.1 = (bf16[256,1024]{1,0:T(8,128)(2,1)S(1)}, bf16[256,1024]{1,0:T(8,128)(2,1)}, u32[]{:S(2)}) copy-start(bf16[256,1024]{1,0:T(8,128)(2,1)} %param.12) | copy-start | bytes 1572868
  23.5 11.8 %copy-start.4 = (s32[256]{0:T(256)S(1)}, s32[256]{0:T(256)}, u32[]{:S(2)}) copy-start(s32[256]{0:T(256)} %param.11) | copy-start | bytes 3076
  30.3 26.2 %all-to-all-start = ((bf16[32,6,2048]{2,1,0:T(8,128)(2,1)}), bf16[32,6,2048]{2,1,0:T(8,128)(2,1)S(1)}, u32[]{:S(2)}, u32[]{:S(2)}) async-start(bf16[32,6,2048]{2,1,0:T(8,128)(2,1)} %reshape.98), calls=%async_computation | async-start | bytes 2097152 | tf_op jit(solution)/shard_map/all_to_all | solution.py:37
  34.2 327.8 %reduce-scatter.4.cloned.1.call-start = ((), (), s32[]{:S(2)}) async-start(), calls=%async_computation.4 | async-start | bytes 8650752
  61.9 1.0 copy-start.2
  62.9 1.0 copy-start.3
Sparse Core Ops, SparseCore 0:
  115.5 246.4 reduce-scatter.3
where the time goes:
time: 456 us; the launch traced here: 453 us
  waiting for transfers between devices  266 us (58%)
  blocking collectives  111 us (24%)
  matrix products  22.3 us (5%)
  local copies, waits for them, and re-layouts  22.1 us (5%)
  starting transfers between devices  14.5 us (3%)
  between operations  14.3 us (3%)
    unnamed x2, waiting for transfers between devices  238 us
    psum x1, blocking collectives, shards(): kv_weight_grad = lax.psum(shares, 'dp')  81.8 us
    all_to_all x1, blocking collectives, shards(): lax.all_to_all(slot_grad.reshape(peers, capacity, -1), 'seq', split_axis=...  29.1 us
    all_to_all x1, waiting for transfers between devices, shards(): lax.all_to_all(spread(enc).reshape(peers, capacity, -1), 'seq', split_axi...  20.9 us
    unnamed x16, local copies, waits for them, and re-layouts  18 us
    all_to_all x1, starting transfers between devices, shards(): lax.all_to_all(label_out, 'seq', split_axis=0, concat_axis=0, tiled=True)  10.5 us
  transfers between devices with their start and end apart: 3, of which 3 were waited for; matrix products, arithmetic and copies ran while one was open for 3% of the time, Pallas kernels for 0%

commit v1 on v0

--- a/solution.py
+++ b/solution.py
@@ -7,42 +7,45 @@
 
 HEADS = 8
 HEAD_DIM = 128
+LANES = 128
 
 
 def shards(enc, enc_dest, enc_group, query, dec_group, out_grad, w_kv):
     peers = lax.axis_size("seq")
-    enc_rows = enc.shape[0]
+    groups = lax.axis_size("dp")
+    enc_rows, model = enc.shape
     capacity = 3 * enc_rows // (2 * peers)
     slot_count = peers * capacity
-    width = w_kv.shape[1] // 2
+    full = w_kv.shape[1]
+    width = full // 2
     dec_rows = query.shape[0]
     scale = 1.0 / math.sqrt(HEAD_DIM)
-    norm_factor = 1.0 / math.sqrt(enc_rows * peers * lax.axis_size("dp"))
+    norm_factor = 1.0 / math.sqrt(enc_rows * peers * groups)
+    block = -(-full // (groups * 8)) * 8
+    share = model // peers
+    packed_rows = capacity * model // LANES
+
+    enc_all = lax.all_gather(enc, "dp", axis=0, tiled=True)
+
     dest = enc_dest[:, 0]
     hits = (dest[:, None] == jnp.arange(peers, dtype=jnp.int32)[None, :]).astype(jnp.int32)
     before = jnp.cumsum(hits, axis=0) - hits
     rank = jnp.sum(before * hits, axis=1)
     target = dest * capacity + rank
-    placing = (target[:, None] == jnp.arange(slot_count, dtype=jnp.int32)[None, :]).astype(
-        jnp.bfloat16
-    )
+    placed = target[:, None] == jnp.arange(slot_count, dtype=jnp.int32)[None, :]
+    placing = placed.astype(jnp.bfloat16)
+    slots = lax.dot_general(
+        placing, enc, (((0,), (0,)), ((), ())), preferred_element_type=jnp.float32
+    ).astype(jnp.bfloat16)
+    label_out = jnp.sum(jnp.where(placed, (enc_group + 1)[:, None], 0), axis=0)
+    label_out = label_out.astype(jnp.bfloat16).reshape(peers, 1, capacity)
+    label_out = jnp.pad(label_out, ((0, 0), (0, 7), (0, LANES - capacity)))
+    outgoing = jnp.concatenate([slots.reshape(peers, packed_rows, LANES), label_out], axis=1)
+    incoming = lax.all_to_all(outgoing, "seq", split_axis=0, concat_axis=0, tiled=True)
+    received = incoming[:, :packed_rows].reshape(slot_count, model)
+    labels = incoming[:, packed_rows, :capacity].reshape(slot_count).astype(jnp.float32)
 
-    def spread(rows):
-        return lax.dot_general(
-            placing, rows, (((0,), (0,)), ((), ())), preferred_element_type=jnp.float32
-        ).astype(jnp.bfloat16)
-
-    label_out = spread((enc_group + 1).astype(jnp.bfloat16)[:, None]).reshape(peers, capacity)
-    sent, label_in = (
-        lax.all_to_all(
-            spread(enc).reshape(peers, capacity, -1), "seq", split_axis=0, concat_axis=0, tiled=True
-        ),
-        lax.all_to_all(label_out, "seq", split_axis=0, concat_axis=0, tiled=True),
-    )
-    slot_kv = jnp.dot(
-        sent.reshape(slot_count, -1), w_kv, preferred_element_type=jnp.float32
-    ).astype(jnp.bfloat16)
-    labels = label_in.reshape(slot_count).astype(jnp.float32)
+    slot_kv = jnp.dot(received, w_kv, preferred_element_type=jnp.float32).astype(jnp.bfloat16)
     allowed = (labels[None, :] == (dec_group + 1).astype(jnp.float32)[:, None])[None]
     queries = query.reshape(dec_rows, HEADS, HEAD_DIM)
     grads_in = out_grad.reshape(dec_rows, HEADS, HEAD_DIM)
@@ -70,22 +73,27 @@
     ).reshape(slot_count, width)
     slot_grad = jnp.concatenate([key_grad, value_grad], axis=1).astype(jnp.bfloat16)
     returned = lax.all_to_all(
-        slot_grad.reshape(peers, capacity, -1), "seq", split_axis=0, concat_axis=0, tiled=True
-    )
-    kv_grad = jnp.dot(
-        placing, returned.reshape(slot_count, -1), preferred_element_type=jnp.float32
+        slot_grad.reshape(peers, packed_rows, LANES), "seq", split_axis=0, concat_axis=0, tiled=True
+    ).reshape(slot_count, full)
+
+    columns = lax.dot_general(
+        returned, placing, (((0,), (1,)), ((), ())), preferred_element_type=jnp.float32
     ).astype(jnp.bfloat16)
     enc_grad = lax.dot_general(
-        kv_grad, w_kv, (((1,), (1,)), ((), ())), preferred_element_type=jnp.float32
+        columns, w_kv, (((0,), (1,)), ((), ())), preferred_element_type=jnp.float32
     ).astype(jnp.bfloat16)
-    partial_value = (
-        lax.dot_general(enc, kv_grad, (((0,), (0,)), ((), ())), preferred_element_type=jnp.float32)
-        * norm_factor
-    )
-    shares = lax.psum_scatter(
-        partial_value.astype(jnp.bfloat16), "seq", scatter_dimension=0, tiled=True
-    ).astype(jnp.float32)
-    kv_weight_grad = lax.psum(shares, "dp")
+
+    blocks = jnp.pad(columns, ((0, groups * block - full), (0, 0))).reshape(groups, block, enc_rows)
+    blocks = lax.all_to_all(blocks, "dp", split_axis=0, concat_axis=0, tiled=True)
+    blocks = blocks.transpose(1, 0, 2).reshape(block, groups * enc_rows)
+    part = jnp.dot(blocks, enc_all, preferred_element_type=jnp.float32) * norm_factor
+    part = part.astype(jnp.bfloat16).reshape(2, block // 2, peers, share)
+    part = part.transpose(2, 1, 0, 3).reshape(peers, block // 2, 2 * share)
+    parts = lax.all_to_all(part, "seq", split_axis=0, concat_axis=0, tiled=True)
+    total = jnp.sum(parts.astype(jnp.float32), axis=0).astype(jnp.bfloat16)
+    totals = lax.all_gather(total, "dp", axis=0, tiled=False)
+    totals = totals.reshape(groups, block // 2, 2, share).transpose(3, 0, 2, 1)
+    kv_weight_grad = totals.reshape(share, groups * block)[:, :full].astype(jnp.float32)
     return (query_grad, enc_grad, kv_weight_grad)
 
 

time: 456 us -> 190 us (0.42)
  waiting for transfers between devices: 266 us -> 22.6 us
  local copies, waits for them, and re-layouts: 22.1 us -> 8.68 us
  blocking collectives: 111 us -> 98.7 us
    unnamed x2 -> x1, waiting for transfers between devices: 238 us -> 0.68 us
    psum x1 -> x0, blocking collectives: 81.8 us -> none  [shards(): kv_weight_grad = lax.psum(shares, 'dp')]
    all_to_all x1 -> x2, blocking collectives: 29.1 us -> 71.1 us  [the longest x1 46.2 us: shards(): lax.all_to_all(blocks, 'dp', split_axis=0, concat_axis=0, tiled=True)]
    all_gather x0 -> x1, blocking collectives: none -> 27.6 us  [shards(): totals = lax.all_gather(total, 'dp', axis=0, tiled=False)]
    unnamed x16 -> x13, local copies, waits for them, and re-layouts: 18 us -> 2.2 us
    all_to_all x2, waiting for transfers between devices: 27.6 us -> 22 us  [the longest x1 18.9 us: shards(): lax.all_to_all(outgoing, 'seq', split_axis=0, concat_axis=0, tiled=True)]
    dot_general x6 -> x5, matrix products: 19.5 us -> 21.1 us  [the longest x1 7.1 us: shards(): lax.dot_general(columns, w_kv, (((0,), (1,)), ((), ())), preferred_elemen...]
  transfers between devices with their start and end apart: 3 -> 3, of which waited for: 3 -> 2; matrix products, arithmetic and copies ran while one was open for 3% -> 13% of each run, Pallas kernels for 0% -> 0%
where the time goes in v1:
time: 190 us; the launch traced here: 189 us
  blocking collectives  98.7 us (52%)
  matrix products  23.8 us (13%)
  waiting for transfers between devices  22.6 us (12%)
  starting transfers between devices  15.3 us (8%)
  between operations  14.4 us (8%)
  local copies, waits for them, and re-layouts  8.68 us (5%)
  other arithmetic  5.64 us (3%)
    all_to_all x1, blocking collectives, shards(): lax.all_to_all(blocks, 'dp', split_axis=0, concat_axis=0, tiled=True)  46.2 us
    all_gather x1, blocking collectives, shards(): totals = lax.all_gather(total, 'dp', axis=0, tiled=False)  27.6 us
    all_to_all x1, blocking collectives, shards(): lax.all_to_all(slot_grad.reshape(peers, packed_rows, LANES), 'seq', split...  24.9 us
    all_to_all x1, waiting for transfers between devices, shards(): lax.all_to_all(outgoing, 'seq', split_axis=0, concat_axis=0, tiled=True)  18.9 us
    all_to_all x1, starting transfers between devices, shards(): lax.all_to_all(outgoing, 'seq', split_axis=0, concat_axis=0, tiled=True)  10.6 us
    dot_general x1, matrix products, shards(): lax.dot_general(columns, w_kv, (((0,), (1,)), ((), ())), preferred_elemen...  7.1 us
    dot_general x1, matrix products, shards(): jnp.dot(blocks, enc_all, preferred_element_type=jnp.float32) * norm_factor  6.72 us
    dot_general x1, matrix products, shards(): jnp.dot(received, w_kv, preferred_element_type=jnp.float32)  5.35 us
  transfers between devices with their start and end apart: 3, of which 2 were waited for; matrix products, arithmetic and copies ran while one was open for 13% of the time, Pallas kernels for 0%

profile of v1, /device:TPU:1, one launch (start us, length us, event | category | flops | bytes accessed | tf_op | source)
XLA Modules:
  0.0 189.2 jit_solution(6630716589970073253)
XLA Ops:
  7.2 0.7 all-gather.4.cloned.1.call-update
  7.9 0.7 fusion.30
  8.8 0.8 select_reduce_fusion.1
  9.7 0.7 broadcast_add_fusion
  11.2 1.4 convolution_convert_fusion.1
  13.0 1.0 fusion.13
  14.1 10.6 %all-to-all-start = ((bf16[32,104,128]{2,1,0:T(8,128)(2,1)}), bf16[32,104,128]{2,1,0:T(8,128)(2,1)S(1)}, u32[]{:S(2)}, u32[]{:S(2)}) async-start(bf16[32,104,128]{2,1,0:T(8,128)(2,1)} %fusion.13), calls=%async_computation | async-start | bytes 1703936 | tf_op jit(solution)/shard_map/all_to_all | solution.py:44
  24.9 18.9 %all-to-all-done = bf16[32,104,128]{2,1,0:T(8,128)(2,1)S(1)} async-done(((bf16[32,104,128]{2,1,0:T(8,128)(2,1)}), bf16[32,104,128]{2,1,0:T(8,128)(2,1)S(1)}, u32[]{:S(2)}, u32[]{:S(2)}) %all-to-all-start) | async-done | bytes 852000 | tf_op jit(solution)/shard_map/all_to_all | solution.py:44
  44.5 5.4 %convolution_convert_fusion = bf16[192,2048]{1,0:T(8,128)(2,1)S(1)} fusion(bf16[192,2048]{1,0:T(8,128)(2,1)S(1)} %reshape.121, bf16[2048,2048]{1,0:T(8,128)(2,1)} %param.13), kind=kOutput, calls=%fused_computation | convolution fusion | flops 1611005952 | bytes 9961472 | tf_op jit(solution)/shard_map/dot_general | solution.py:48
  51.9 0.9 copy-done.1
  54.2 24.9 %all_to_all.20 = bf16[32,96,128]{2,1,0:T(8,128)(2,1)S(1)} all-to-all(bf16[32,96,128]{2,1,0:T(8,128)(2,1)S(1)} %convert_element_type.91), channel_id=1, replica_groups=mesh['dp'=24,'seq'=32] {'seq'}, dimensions={0} | all-to-all | bytes 1572864 | tf_op jit(solution)/shard_map/all_to_all | solution.py:75
  80.0 46.2 %all_to_all.21 = bf16[24,88,128]{2,1,0:T(8,128)(2,1)S(1)} all-to-all(bf16[24,88,128]{2,1,0:T(8,128)(2,1)S(1)} %bitcast.116), channel_id=1, replica_groups=mesh['dp'=24,'seq'=32] {'dp'}, dimensions={0} | all-to-all | bytes 1081344 | tf_op jit(solution)/shard_map/all_to_all | solution.py:87
  126.2 6.7 %fusion = bf16[88,2048]{1,0:T(8,128)(2,1)S(1)} fusion(bf16[3072,2048]{1,0:T(8,128)(2,1)} %all-gather.4.cloned.1.call-done, bf16[24,88,128]{2,1,0:T(8,128)(2,1)S(1)} %all_to_all.21), kind=kOutput, calls=%fused_computation.5 | convolution fusion | flops 1107656704 | bytes 13484032 | tf_op jit(solution)/shard_map/dot_general | solution.py:89
  132.9 0.7 reshape.131
  133.6 0.7 copy.134
  134.7 0.9 copy.86
  135.6 4.6 %all-to-all-start.3 = ((bf16[32,44,128]{2,1,0:T(8,128)(2,1)}), bf16[32,44,128]{2,1,0:T(8,128)(2,1)S(1)}, u32[]{:S(2)}, u32[]{:S(2)}) async-start(bf16[32,44,128]{2,1,0:T(8,128)(2,1)} %copy.86), calls=%async_computation.3 | async-start | bytes 786432 | tf_op jit(solution)/shard_map/all_to_all | solution.py:92
  140.6 1.0 copy.89
  141.6 7.1 %convolution_convert_fusion.2 = bf16[128,2048]{1,0:T(8,128)(2,1)} fusion(bf16[2048,128]{1,0:T(8,128)(2,1)S(1)} %convolution_convert_fusion.3, bf16[2048,2048]{1,0:T(8,128)(2,1)} %param.13), kind=kOutput, calls=%fused_computation.2 | convolution fusion | flops 1074003968 | bytes 9437184 | tf_op jit(solution)/shard_map/dot_general | solution.py:82
  148.7 3.1 %all-to-all-done.3 = bf16[32,44,128]{2,1,0:T(8,128)(2,1)S(1)} async-done(((bf16[32,44,128]{2,1,0:T(8,128)(2,1)}), bf16[32,44,128]{2,1,0:T(8,128)(2,1)S(1)}, u32[]{:S(2)}, u32[]{:S(2)}) %all-to-all-start.3) | async-done | bytes 360480 | tf_op jit(solution)/shard_map/all_to_all | solution.py:92
  151.9 27.6 %all-gather.1 = bf16[24,44,128]{2,1,0:T(8,128)(2,1)S(1)} all-gather(bf16[1,44,128]{2,1,0:T(8,128)(2,1)S(1)} %bitcast.121), channel_id=2, replica_groups=mesh['dp'=24,'seq'=32] {'dp'}, dimensions={0}, use_global_device_ids=true | all-gather | bytes 281600 | tf_op jit(solution)/shard_map/all_gather | solution.py:94
  179.8 0.9 copy.88
  180.8 0.7 reshape.134
  181.5 0.8 slice_convert_fusion
  (44 shorter events, 7.5 us)
Async XLA Ops:
  7.2 42.7 %copy-start = (bf16[256,1024]{1,0:T(8,128)(2,1)S(1)}, bf16[256,1024]{1,0:T(8,128)(2,1)}, u32[]{:S(2)}) copy-start(bf16[256,1024]{1,0:T(8,128)(2,1)} %param.10) | copy-start | bytes 1572868
  7.2 119.0 %all-gather.4.cloned.1.call-start = ((), (), s32[]{:S(2)}) async-start(), calls=%async_computation.4 | async-start | bytes 13107200 | tf_op jit(solution)/shard_map/all_gather | solution.py:28
  13.0 11.7 %copy-start.3 = (bf16[256,1024]{1,0:T(8,128)(2,1)S(1)}, bf16[256,1024]{1,0:T(8,128)(2,1)}, u32[]{:S(2)}) copy-start(bf16[256,1024]{1,0:T(8,128)(2,1)} %param.12) | copy-start | bytes 1572868
  14.1 10.9 %copy-start.4 = (s32[256]{0:T(256)S(1)}, s32[256]{0:T(256)}, u32[]{:S(2)}) copy-start(s32[256]{0:T(256)} %param.11) | copy-start | bytes 3076
  14.1 29.8 %all-to-all-start = ((bf16[32,104,128]{2,1,0:T(8,128)(2,1)}), bf16[32,104,128]{2,1,0:T(8,128)(2,1)S(1)}, u32[]{:S(2)}, u32[]{:S(2)}) async-start(bf16[32,104,128]{2,1,0:T(8,128)(2,1)} %fusion.13), calls=%async_computation | async-start | bytes 1703936 | tf_op jit(solution)/shard_map/all_to_all | solution.py:44
  51.8 0.9 copy-start.1
  134.4 5.9 %copy-start.2 = (bf16[8,256,192]{1,2,0:T(8,128)(2,1)S(1)}, bf16[8,256,192]{1,2,0:T(8,128)(2,1)}, u32[]{:S(2)}) copy-start(bf16[8,256,192]{1,2,0:T(8,128)(2,1)} %copy-done.1) | copy-start | bytes 2359300
  135.6 16.2 %all-to-all-start.3 = ((bf16[32,44,128]{2,1,0:T(8,128)(2,1)}), bf16[32,44,128]{2,1,0:T(8,128)(2,1)S(1)}, u32[]{:S(2)}, u32[]{:S(2)}) async-start(bf16[32,44,128]{2,1,0:T(8,128)(2,1)} %copy.86), calls=%async_computation.3 | async-start | bytes 786432 | tf_op jit(solution)/shard_map/all_to_all | solution.py:92
Sparse Core Ops, SparseCore 0:
  10.5 93.3 all-gather.3

commit v2 on v1

v2 whole, which is shorter than its diff:
```python
import functools
import math

import jax
import jax.numpy as jnp
from jax import lax
from jax.experimental import pallas as pl
from jax.experimental.pallas import tpu as pltpu
from jax.sharding import Mesh, PartitionSpec as P

HEADS = 8
HEAD_DIM = 128
LANES = 128
FAR = -1e30
MIB = 1 << 20
IN_FLIGHT = 16
PARTS = 3


def contract(a, b, dims):
    return lax.dot_general(a, b, (dims, ((), ())), preferred_element_type=jnp.float32)


def streamed(source, target, sems):
    count = sems.shape[0]
    rows = source.shape[0] // count
    spans = [pl.ds(k * rows, rows) for k in range(count)]
    copies = [
        pltpu.make_async_copy(source.at[at], target.at[at], sems.at[k]) for k, at in enumerate(spans)
    ]
    for copy in copies[:IN_FLIGHT]:
        copy.start()

    def wait(k):
        copies[k].wait()
        if k + IN_FLIGHT < count:
            copies[k + IN_FLIGHT].start()

    return wait


def product(rows, source, near, sems, total):
    count = sems.shape[0]
    depth = source.shape[0] // count
    wait = streamed(source, near, sems)

    def run():
        for k in range(count):
            wait(k)
            at = slice(k * depth, (k + 1) * depth)
            part = contract(rows[:, at], near[at, :], ((1,), (0,)))
            total[...] = part if k == 0 else total[...] + part

    return run


def turned(row, diagonal):
    return jnp.sum(jnp.where(diagonal, row.astype(jnp.float32), 0.0), axis=1, keepdims=True)


def route_kernel(
    peers,
    capacity,
    stride,
    enc_hbm,
    dest_hbm,
    group_hbm,
    w_hbm,
    out_ref,
    placing_ref,
    enc_ref,
    row_refs,
    w_ref,
    kv,
    wide,
    sems,
    w_sems,
):
    copies = [
        pltpu.make_async_copy(dest_hbm, row_refs.at[0], sems.at[0]),
        pltpu.make_async_copy(group_hbm, row_refs.at[1], sems.at[1]),
        pltpu.make_async_copy(enc_hbm, enc_ref, sems.at[2]),
    ]
    for copy in copies:
        copy.start()
    multiply = product(enc_ref, w_hbm, w_ref, w_sems, kv)
    rows = enc_ref.shape[0]
    chunks = kv.shape[1] // LANES
    ahead = lax.broadcasted_iota(jnp.int32, (rows, rows), 0)
    behind = lax.broadcasted_iota(jnp.int32, (rows, rows), 1)
    earlier = jnp.where(behind < ahead, 1.0, 0.0).astype(jnp.bfloat16)
    copies[0].wait()
    copies[1].wait()
    dest = turned(row_refs[0], ahead == behind).astype(jnp.int32)
    label = turned(row_refs[1] + 1, ahead == behind)
    owner = lax.broadcasted_iota(jnp.int32, (rows, peers), 1)
    hits = jnp.where(owner == dest, 1.0, 0.0)
    before = contract(earlier, hits.astype(jnp.bfloat16), ((1,), (0,)))
    rank = jnp.sum(before * hits, axis=1, keepdims=True).astype(jnp.int32)
    slot = lax.broadcasted_iota(jnp.int32, (rows, peers * capacity), 1)
    placing_ref[...] = jnp.where(slot == dest * capacity + rank, 1.0, 0.0).astype(jnp.bfloat16)
    placing = jnp.where(slot == rank * peers + dest, 1.0, 0.0).astype(jnp.bfloat16)
    lane = lax.broadcasted_iota(jnp.int32, (rows, LANES), 1)
    spots = jnp.where(lane == rank, label, 0.0).astype(jnp.bfloat16)
    labels = contract(hits.astype(jnp.bfloat16), spots, ((0,), (0,)))
    for extra in range(capacity * chunks, stride):
        wide[pl.ds(extra, peers, stride=stride), :] = labels
    copies[2].wait()
    multiply()
    slots = contract(placing, kv[...].astype(jnp.bfloat16), ((0,), (0,)))
    for r in range(capacity):
        for c in range(chunks):
            wide[pl.ds(r * chunks + c, peers, stride=stride), :] = slots[
                r * peers : (r + 1) * peers, c * LANES : (c + 1) * LANES
            ]
    out_ref[...] = wide[...].astype(jnp.bfloat16)


def attention_kernel(
    peers,
    capacity,
    stride,
    incoming_ref,
    group_ref,
    placing_ref,
    query_ref,
    grad_ref,
    query_grad_ref,
    out_ref,
    placing_out_ref,
    wide,
    received,
    bias,
):
    slot_count, model = received.shape
    chunks = model // LANES
    width = HEADS * HEAD_DIM
    scale = 1.0 / math.sqrt(HEAD_DIM)
    placing_out_ref[...] = placing_ref[...]
    wide[...] = incoming_ref[...].astype(jnp.float32)
    for r in range(capacity):
        for c in range(chunks):
            received[r * peers : (r + 1) * peers, c * LANES : (c + 1) * LANES] = wide[
                pl.ds(r * chunks + c, peers, stride=stride), :
            ].astype(jnp.bfloat16)
    labels = wide[pl.ds(capacity * chunks, peers, stride=stride), :]
    group = group_ref[...].astype(jnp.float32) + 1.0
    for r in range(capacity):
        bias[r * peers : (r + 1) * peers, :] = jnp.where(labels[:, r : r + 1] == group, 0.0, FAR)

    def columns_of(head):
        return slice(head * HEAD_DIM, (head + 1) * HEAD_DIM)

    def products(head):
        at, of_values = columns_of(head), columns_of(HEADS + head)
        score = contract(received[:, at], query_ref[:, at], ((1,), (1,))) * scale + bias[...]
        value_dot = contract(received[:, of_values], grad_ref[:, at], ((1,), (1,)))
        return score, value_dot

    def softmax(score, value_dot):
        top = jnp.maximum(jnp.max(score, axis=0, keepdims=True), 0.0)
        expo = jnp.exp(score - top)
        weight = expo * (1.0 / (jnp.exp(-top) + jnp.sum(expo, axis=0, keepdims=True)))
        probs = weight.astype(jnp.bfloat16)
        delta = jnp.sum(probs.astype(jnp.float32) * value_dot, axis=0, keepdims=True)
        return probs, (weight * ((value_dot - delta) * scale)).astype(jnp.bfloat16)

    def gradients(head, probs, score_grad):
        at = columns_of(head)
        key_grad = contract(score_grad, query_ref[:, at], ((1,), (0,)))
        value_grad = contract(probs, grad_ref[:, at], ((1,), (0,)))
        query_grad_ref[:, at] = contract(score_grad, received[:, at], ((0,), (0,))).astype(jnp.bfloat16)
        for r in range(capacity):
            rows = slice(r * peers, (r + 1) * peers)
            for c, part in ((head, key_grad), (HEADS + head, value_grad)):
                wide[pl.ds(r * chunks + c, peers, stride=capacity * chunks), :] = part[rows]

    scores, weights = {}, {}
    for turn in range(HEADS + 2):
        if turn < HEADS:
            scores[turn] = products(turn)
        if 0 <= turn - 1 < HEADS:
            weights[turn - 1] = softmax(*scores.pop(turn - 1))
        if turn >= 2:
            gradients(turn - 2, *weights.pop(turn - 2))
    out_ref[...] = wide[: slot_count * chunks, :].astype(jnp.bfloat16)


def columns_kernel(returned_ref, placing_ref, out_ref, wide):
    wide[...] = returned_ref[...].astype(jnp.float32)
    slot_count = placing_ref.shape[1]
    chunks = returned_ref.shape[0] // slot_count
    for c in range(chunks):
        rows = wide[pl.ds(c, slot_count, stride=chunks), :].astype(jnp.bfloat16)
        turned_rows = contract(rows, placing_ref[...], ((0,), (1,)))
        out_ref[c * LANES : (c + 1) * LANES, :] = turned_rows.astype(jnp.bfloat16)
    extra = out_ref.shape[0] - chunks * LANES
    if extra:
        out_ref[chunks * LANES :, :] = jnp.zeros((extra, out_ref.shape[1]), jnp.bfloat16)


def tile_kernel(block, share, norm_factor, blocks_ref, enc_hbm, out_ref, rows, near, total, sems):
    multiply = product(rows, enc_hbm, near, sems, total)
    groups, enc_rows = blocks_ref.shape[0], blocks_ref.shape[2]
    for g in range(groups):
        rows[:, g * enc_rows : (g + 1) * enc_rows] = blocks_ref[g]
    multiply()
    kept = out_ref.shape[1]
    low = lax.broadcasted_iota(jnp.int32, (kept, LANES), 1) < share
    for p in range(total.shape[1] // LANES):
        two = total[:, p * LANES : (p + 1) * LANES] * norm_factor
        first, second = two[:kept], two[block - kept :]
        out_ref[2 * p] = jnp.where(low, first, pltpu.roll(second, share, 1)).astype(jnp.bfloat16)
        out_ref[2 * p + 1] = jnp.where(low, pltpu.roll(first, share, 1), second).astype(jnp.bfloat16)


def sum_kernel(block, share, parts_ref, out_ref):
    kept = parts_ref.shape[1]
    total = parts_ref[0].astype(jnp.float32)
    for i in range(1, parts_ref.shape[0]):
        total += parts_ref[i].astype(jnp.float32)
    columns = total.T
    pieces = [columns[:share], columns[share:, 2 * kept - block :]]
    extra = out_ref.shape[1] - block
    if extra:
        pieces.append(jnp.zeros((share, extra), jnp.float32))
    out_ref[...] = jnp.concatenate(pieces, axis=1).astype(jnp.bfloat16)


def join_kernel(totals_ref, out_ref):
    total = totals_ref[0].astype(jnp.float32)
    for t in range(1, totals_ref.shape[0]):
        total += totals_ref[t].astype(jnp.float32)
    shared = total.astype(jnp.bfloat16)
    for g in range(out_ref.shape[0]):
        out_ref[g] = shared


def final_kernel(block, totals_ref, out_ref):
    full = out_ref.shape[1]
    for g in range(totals_ref.shape[0]):
        end = min((g + 1) * block, full)
        out_ref[:, g * block : end] = totals_ref[g, :, : end - g * block].astype(jnp.float32)


def shards(enc, enc_dest, enc_group, query, dec_group, out_grad, w_kv):
    peers = lax.axis_size("seq")
    parts = lax.axis_size("part")
    groups = lax.axis_size("group")
    enc_rows, model = enc.shape
    capacity = 3 * enc_rows // (2 * peers)
    slot_count = peers * capacity
    full = w_kv.shape[1]
    width = full // 2
    dec_rows = query.shape[0]
    norm_factor = 1.0 / math.sqrt(enc_rows * peers * groups * parts)
    block = -(-full // (groups * 8)) * 8
    kept = -(-block // 32) * 16
    block_lanes = -(-block // LANES) * LANES
    share = model // peers
    chunks = full // LANES
    packed_rows = capacity * chunks
    stride = packed_rows + 8

    enc_all = lax.all_gather(enc, "group", axis=0, tiled=True)

    outgoing, placing = pl.pallas_call(
        functools.partial(route_kernel, peers, capacity, stride),
        out_shape=(
            jax.ShapeDtypeStruct((peers * stride, LANES), jnp.bfloat16),
            jax.ShapeDtypeStruct((enc_rows, slot_count), jnp.bfloat16),
        ),
        in_specs=[pl.BlockSpec(memory_space=pltpu.HBM)] * 4,
        scratch_shapes=[
            pltpu.VMEM((enc_rows, model), jnp.bfloat16),
            pltpu.VMEM((2, 1, enc_rows), jnp.int32),
            pltpu.VMEM((model, full), jnp.bfloat16),
            pltpu.VMEM((enc_rows, full), jnp.float32),
            pltpu.VMEM((peers * stride, LANES), jnp.float32),
            pltpu.SemaphoreType.DMA((3,)),
            pltpu.SemaphoreType.DMA((4,)),
        ],
        compiler_params=pltpu.CompilerParams(vmem_limit_bytes=64 * MIB),
    )(enc, enc_dest.reshape(1, enc_rows), enc_group.reshape(1, enc_rows), w_kv)
    incoming = lax.all_to_all(
        outgoing.reshape(peers, stride, LANES), "seq", split_axis=0, concat_axis=0, tiled=True
    )

    query_grad, slot_grad, placing = pl.pallas_call(
        functools.partial(attention_kernel, peers, capacity, stride),
        out_shape=(
            jax.ShapeDtypeStruct((dec_rows, width), jnp.bfloat16),
            jax.ShapeDtypeStruct((peers * packed_rows, LANES), jnp.bfloat16),
            jax.ShapeDtypeStruct((enc_rows, slot_count), jnp.bfloat16),
        ),
        scratch_shapes=[
            pltpu.VMEM((peers * stride, LANES), jnp.float32),
            pltpu.VMEM((slot_count, full), jnp.bfloat16),
            pltpu.VMEM((slot_count, dec_rows), jnp.float32),
        ],
        compiler_params=pltpu.CompilerParams(vmem_limit_bytes=60 * MIB),
    )(
        incoming.reshape(peers * stride, LANES),
        dec_group.reshape(1, dec_rows),
        placing,
        query,
        out_grad,
    )
    returned = lax.all_to_all(
        slot_grad.reshape(peers, packed_rows, LANES), "seq", split_axis=0, concat_axis=0, tiled=True
    )

    columns = pl.pallas_call(
        columns_kernel,
        out_shape=jax.ShapeDtypeStruct((groups * block, enc_rows), jnp.bfloat16),
        scratch_shapes=[pltpu.VMEM((peers * packed_rows, LANES), jnp.float32)],
        compiler_params=pltpu.CompilerParams(vmem_limit_bytes=32 * MIB),
    )(returned.reshape(peers * packed_rows, LANES), placing)
    enc_grad = contract(columns[:full], w_kv, ((0,), (1,))).astype(jnp.bfloat16)

    blocks = lax.all_to_all(
        columns.reshape(groups, block, enc_rows), "group", split_axis=0, concat_axis=0, tiled=True
    )
    tile = pl.pallas_call(
        functools.partial(tile_kernel, block, share, norm_factor),
        out_shape=jax.ShapeDtypeStruct((peers, kept, 2 * share), jnp.bfloat16),
        in_specs=[pl.BlockSpec(memory_space=pltpu.VMEM), pl.BlockSpec(memory_space=pltpu.HBM)],
        scratch_shapes=[
            pltpu.VMEM((block, groups * enc_rows), jnp.bfloat16),
            pltpu.VMEM((groups * enc_rows, model), jnp.bfloat16),
            pltpu.VMEM((block, model), jnp.float32),
            pltpu.SemaphoreType.DMA((groups // 2,)),
        ],
        compiler_params=pltpu.CompilerParams(vmem_limit_bytes=62 * MIB),
    )(blocks, enc_all)
    tiles = lax.all_to_all(tile, "seq", split_axis=0, concat_axis=0, tiled=True)
    shared = pl.pallas_call(
        functools.partial(sum_kernel, block, share),
        out_shape=jax.ShapeDtypeStruct((share, block_lanes), jnp.bfloat16),
        compiler_params=pltpu.CompilerParams(vmem_limit_bytes=32 * MIB),
    )(tiles)
    shared = lax.all_gather(shared, "part", axis=0, tiled=True).reshape(parts, share, block_lanes)
    shared = pl.pallas_call(
        join_kernel,
        out_shape=jax.ShapeDtypeStruct((groups, share, block_lanes), jnp.bfloat16),
        compiler_params=pltpu.CompilerParams(vmem_limit_bytes=32 * MIB),
    )(shared)
    shared = lax.all_to_all(shared, "group", split_axis=0, concat_axis=0, tiled=True)
    kv_weight_grad = pl.pallas_call(
        functools.partial(final_kernel, block),
        out_shape=jax.ShapeDtypeStruct((share, full), jnp.float32),
        compiler_params=pltpu.CompilerParams(vmem_limit_bytes=32 * MIB),
    )(shared)
    return (query_grad, enc_grad, kv_weight_grad)


def solution(mesh):
    dp, seq = mesh.devices.shape
    cut = Mesh(mesh.devices.reshape(PARTS, dp // PARTS, seq), ("part", "group", "seq"))
    rows = ("part", "group", "seq")
    in_specs = (P(rows, None), P(rows, None), P(rows), P(rows, None), P(rows), P(rows, None), P())
    out_specs = (P(rows, None), P(rows, None), P("seq", None))
    return jax.shard_map(shards, mesh=cut, in_specs=in_specs, out_specs=out_specs, check_vma=False)
```

time: 190 us -> 185 us (0.974)
  blocking collectives: 98.7 us -> 133 us
  waiting for transfers between devices: 22.6 us -> 2.31 us
  Pallas kernels: 0 us -> 19 us
  matrix products: 23.8 us -> 7.1 us
  local copies, waits for them, and re-layouts: 8.68 us -> 0.84 us
  starting transfers between devices: 15.3 us -> 8.44 us
  other arithmetic: 5.64 us -> 0 us
    all_to_all x1 -> x3, blocking collectives: 46.2 us -> 90.3 us  [the longest x1 30.5 us: shards(): lax.all_to_all(columns.reshape(groups, block, enc_rows), 'group', split_a...]
    all_to_all x2 -> x1, waiting for transfers between devices: 22 us -> 1.63 us  [shards(): lax.all_to_all(shared, 'group', split_axis=0, concat_axis=0, tiled=True)]
    pallas_call x0 -> x7, Pallas kernels: none -> 19 us  [the longest x1 5.77 us: shards(): pl.pallas_call(functools.partial(attention_kernel, peers, capacity, strid...]
    dot_general x11 -> x1, matrix products: 23.8 us -> 7.1 us  [contract(): lax.dot_general(a, b, (dims, ((), ())), preferred_element_type=jnp.float32)]
    all_gather x1, blocking collectives: 27.6 us -> 18.2 us  [shards(): lax.all_gather(shared, 'part', axis=0, tiled=True)]
    all_to_all x2 -> x1, starting transfers between devices: 15.3 us -> 8.4 us  [shards(): lax.all_to_all(shared, 'group', split_axis=0, concat_axis=0, tiled=True)]
    reshape x10 -> x0, local copies, waits for them, and re-layouts: 4.79 us -> none  [the longest x2 1.49 us: shards(): part = part.astype(jnp.bfloat16).reshape(2, block // 2, peers, share)]
  transfers between devices with their start and end apart: 3 -> 2, of which waited for: 2 -> 1; matrix products, arithmetic and copies ran while one was open for 13% -> 4% of each run, Pallas kernels for 0% -> 7%
where the time goes in v2:
time: 185 us
  blocking collectives  133 us (72%)
  Pallas kernels  19 us (10%)
  between operations  14.1 us (8%)
  starting transfers between devices  8.44 us (5%)
  matrix products  7.1 us (4%)
  waiting for transfers between devices  2.31 us (1%)
    all_to_all x1, blocking collectives, shards(): lax.all_to_all(columns.reshape(groups, block, enc_rows), 'group', split_a...  30.5 us
    all_to_all x1, blocking collectives, shards(): tiles = lax.all_to_all(tile, 'seq', split_axis=0, concat_axis=0, tiled=True)  30.5 us
    all_to_all x1, blocking collectives, shards(): lax.all_to_all(outgoing.reshape(peers, stride, LANES), 'seq', split_axis=...  29.4 us
    all_to_all x1, blocking collectives, shards(): lax.all_to_all(slot_grad.reshape(peers, packed_rows, LANES), 'seq', split...  24.5 us
    all_gather x1, blocking collectives, shards(): lax.all_gather(shared, 'part', axis=0, tiled=True)  18.2 us
    all_to_all x1, starting transfers between devices, shards(): lax.all_to_all(shared, 'group', split_axis=0, concat_axis=0, tiled=True)  8.4 us
    dot_general x1, matrix products, contract(): lax.dot_general(a, b, (dims, ((), ())), preferred_element_type=jnp.float32)  7.1 us
    pallas_call x1, Pallas kernels, shards(): pl.pallas_call(functools.partial(attention_kernel, peers, capacity, strid...  5.77 us
  transfers between devices with their start and end apart: 2, of which 1 were waited for; matrix products, arithmetic and copies ran while one was open for 4% of the time, Pallas kernels for 7%

profile of v2, /device:TPU:1, one launch (start us, length us, event | category | flops | bytes accessed | tf_op | source)
XLA Modules:
  0.0 184.8 jit_solution(5784959400755701015)
XLA Ops:
  7.2 0.0 all-gather.2.cloned.1.call-start
  7.2 0.7 all-gather.2.cloned.1.call-update
  7.9 5.7 %shard_map.94 = (bf16[3328,128]{1,0:T(8,128)(2,1)}, bf16[128,192]{1,0:T(8,128)(2,1)}) custom-call(bf16[128,2048]{1,0:T(8,128)(2,1)} %enc_hbm.1, s32[1,128]{1,0:T(1,128)} %bitcast.18, s32[1,128]{1,0:T(1,128)} %bitcast.19, bf16[2048,2048]{1,0:T(8,128)(2,1)} %w_hbm.1), custom_call_target="tpu_custom_call" | custom-call | tf_op jit(solution)/shard_map/pallas_call | solution.py:267
  13.6 29.4 %all_to_all.25 = bf16[32,104,128]{2,1,0:T(8,128)(2,1)} all-to-all(bf16[32,104,128]{2,1,0:T(8,128)(2,1)} %bitcast.15), channel_id=1, replica_groups=mesh['part'=3,'group'=8,'seq'=32] {'seq'}, dimensions={0} | all-to-all | bytes 1703936 | tf_op jit(solution)/shard_map/all_to_all | solution.py:285
  43.0 5.8 %shard_map.95 = (bf16[256,1024]{1,0:T(8,128)(2,1)}, bf16[3072,128]{1,0:T(8,128)(2,1)}, bf16[128,192]{1,0:T(8,128)(2,1)}) custom-call(bf16[3328,128]{1,0:T(8,128)(2,1)} %bitcast.14, s32[1,256]{1,0:T(1,128)} %bitcast.17, bf16[128,192]{1,0:T(8,128)(2,1)} %get-tuple-element.9.placing_ref, bf16[256,1024]{1,0:T(8,128)(2,1)} %query_ref.1, bf16[256,1024]{1,0:T(8,128)(2,1)} %grad_ref.1), custom_call_target="tpu_custom_call" | custom-call | tf_op jit(solution)/shard_map/pallas_call | solution.py:289
  48.8 24.5 %all_to_all.26 = bf16[32,96,128]{2,1,0:T(8,128)(2,1)S(1)} all-to-all(bf16[32,96,128]{2,1,0:T(8,128)(2,1)} %bitcast.16), channel_id=1, replica_groups=mesh['part'=3,'group'=8,'seq'=32] {'seq'}, dimensions={0} | all-to-all | bytes 1572864 | tf_op jit(solution)/shard_map/all_to_all | solution.py:309
  73.3 0.0 copy-start
  73.3 0.8 copy-done
  74.1 0.9 shard_map.96
  75.0 30.5 %all_to_all.27.blocks_ref = bf16[8,256,128]{2,1,0:T(8,128)(2,1)} all-to-all(bf16[8,256,128]{2,1,0:T(8,128)(2,1)S(1)} %bitcast.11), channel_id=1, replica_groups=mesh['part'=3,'group'=8,'seq'=32] {'group'}, dimensions={0} | all-to-all | bytes 1048576 | tf_op jit(solution)/shard_map/all_to_all | solution.py:321
  105.5 0.0 all-gather.2.cloned.1.call-done.enc_hbm
  105.5 4.8 %shard_map.97 = bf16[32,128,128]{2,1,0:T(8,128)(2,1)} custom-call(bf16[8,256,128]{2,1,0:T(8,128)(2,1)} %all_to_all.27.blocks_ref, bf16[1024,2048]{1,0:T(8,128)(2,1)} %all-gather.2.cloned.1.call-done.enc_hbm), custom_call_target="tpu_custom_call" | custom-call | tf_op jit(solution)/shard_map/pallas_call | solution.py:324
  110.4 30.5 %all_to_all.28.parts_ref = bf16[32,128,128]{2,1,0:T(8,128)(2,1)S(1)} all-to-all(bf16[32,128,128]{2,1,0:T(8,128)(2,1)} %shard_map.97), channel_id=1, replica_groups=mesh['part'=3,'group'=8,'seq'=32] {'seq'}, dimensions={0} | all-to-all | bytes 2097152 | tf_op jit(solution)/shard_map/all_to_all | solution.py:336
  140.8 0.2 shard_map.98
  141.1 18.2 %all_gather.7 = bf16[192,256]{1,0:T(8,128)(2,1)S(1)} all-gather(bf16[64,256]{1,0:T(8,128)(2,1)S(1)} %shard_map.98), channel_id=1, replica_groups=mesh['part'=3,'group'=8,'seq'=32] {'part'}, dimensions={0}, use_global_device_ids=true | all-gather | bytes 131072 | tf_op jit(solution)/shard_map/all_gather | solution.py:342
  159.2 0.7 shard_map.99
  160.0 8.4 %all-to-all-start.4 = ((bf16[8,64,256]{2,1,0:T(8,128)(2,1)}), bf16[8,64,256]{2,1,0:T(8,128)(2,1)S(1)}, u32[]{:S(2)}, u32[]{:S(2)}) async-start(bf16[8,64,256]{2,1,0:T(8,128)(2,1)} %shard_map.99), calls=%async_computation.4 | async-start | bytes 524288 | tf_op jit(solution)/shard_map/all_to_all | solution.py:348
  168.4 7.1 %convolution_convert_fusion = bf16[128,2048]{1,0:T(8,128)(2,1)} fusion(bf16[2048,128]{1,0:T(8,128)(2,1)S(1)} %shard_map.96, bf16[2048,2048]{1,0:T(8,128)(2,1)} %w_hbm.1), kind=kOutput, calls=%fused_computation | convolution fusion | flops 1074003968 | bytes 9437184 | tf_op jit(solution)/shard_map/dot_general | solution.py:21
  175.5 1.6 all-to-all-done.4.totals_ref
  177.1 0.8 shard_map.100
Async XLA Ops:
  7.2 98.4 %all-gather.2.cloned.1.call-start = ((), (), s32[]{:S(2)}) async-start(), calls=%async_computation.5 | async-start | bytes 4718592 | tf_op jit(solution)/shard_map/all_gather | solution.py:265
  73.3 0.8 copy-start
  160.0 17.1 %all-to-all-start.4 = ((bf16[8,64,256]{2,1,0:T(8,128)(2,1)}), bf16[8,64,256]{2,1,0:T(8,128)(2,1)S(1)}, u32[]{:S(2)}, u32[]{:S(2)}) async-start(bf16[8,64,256]{2,1,0:T(8,128)(2,1)} %shard_map.99), calls=%async_computation.4 | async-start | bytes 524288 | tf_op jit(solution)/shard_map/all_to_all | solution.py:348
Sparse Core Ops, SparseCore 0:
  10.4 65.3 all-gather.1

commit v3 on v2

--- a/solution.py
+++ b/solution.py
@@ -13,40 +13,28 @@
 LANES = 128
 FAR = -1e30
 MIB = 1 << 20
-IN_FLIGHT = 16
-PARTS = 3
+LINE = 4
 
 
 def contract(a, b, dims):
     return lax.dot_general(a, b, (dims, ((), ())), preferred_element_type=jnp.float32)
 
 
-def streamed(source, target, sems):
+def product(rows, sources, near, sems, total):
     count = sems.shape[0]
-    rows = source.shape[0] // count
-    spans = [pl.ds(k * rows, rows) for k in range(count)]
+    depth = near.shape[0] // count
+    each = count // len(sources)
+    spans = [pl.ds(k * depth, depth) for k in range(count)]
     copies = [
-        pltpu.make_async_copy(source.at[at], target.at[at], sems.at[k]) for k, at in enumerate(spans)
+        pltpu.make_async_copy(sources[k // each].at[spans[k % each]], near.at[spans[k]], sems.at[k])
+        for k in range(count)
     ]
-    for copy in copies[:IN_FLIGHT]:
+    for copy in copies:
         copy.start()
-
-    def wait(k):
-        copies[k].wait()
-        if k + IN_FLIGHT < count:
-            copies[k + IN_FLIGHT].start()
-
-    return wait
-
-
-def product(rows, source, near, sems, total):
-    count = sems.shape[0]
-    depth = source.shape[0] // count
-    wait = streamed(source, near, sems)
 
     def run():
         for k in range(count):
-            wait(k)
+            copies[k].wait()
             at = slice(k * depth, (k + 1) * depth)
             part = contract(rows[:, at], near[at, :], ((1,), (0,)))
             total[...] = part if k == 0 else total[...] + part
@@ -83,7 +71,7 @@
     ]
     for copy in copies:
         copy.start()
-    multiply = product(enc_ref, w_hbm, w_ref, w_sems, kv)
+    multiply = product(enc_ref, [w_hbm], w_ref, w_sems, kv)
     rows = enc_ref.shape[0]
     chunks = kv.shape[1] // LANES
     ahead = lax.broadcasted_iota(jnp.int32, (rows, rows), 0)
@@ -199,11 +187,13 @@
         out_ref[chunks * LANES :, :] = jnp.zeros((extra, out_ref.shape[1]), jnp.bfloat16)
 
 
-def tile_kernel(block, share, norm_factor, blocks_ref, enc_hbm, out_ref, rows, near, total, sems):
-    multiply = product(rows, enc_hbm, near, sems, total)
+def tile_kernel(
+    block, share, norm_factor, order_ref, blocks_ref, own_hbm, other_hbm, out_ref, rows, near, total, sems
+):
+    multiply = product(rows, [own_hbm, other_hbm], near, sems, total)
     groups, enc_rows = blocks_ref.shape[0], blocks_ref.shape[2]
-    for g in range(groups):
-        rows[:, g * enc_rows : (g + 1) * enc_rows] = blocks_ref[g]
+    for k in range(groups):
+        rows[:, k * enc_rows : (k + 1) * enc_rows] = blocks_ref[order_ref[k]]
     multiply()
     kept = out_ref.shape[1]
     low = lax.broadcasted_iota(jnp.int32, (kept, LANES), 1) < share
@@ -220,33 +210,23 @@
     for i in range(1, parts_ref.shape[0]):
         total += parts_ref[i].astype(jnp.float32)
     columns = total.T
-    pieces = [columns[:share], columns[share:, 2 * kept - block :]]
-    extra = out_ref.shape[1] - block
-    if extra:
-        pieces.append(jnp.zeros((share, extra), jnp.float32))
-    out_ref[...] = jnp.concatenate(pieces, axis=1).astype(jnp.bfloat16)
-
-
-def join_kernel(totals_ref, out_ref):
-    total = totals_ref[0].astype(jnp.float32)
-    for t in range(1, totals_ref.shape[0]):
-        total += totals_ref[t].astype(jnp.float32)
-    shared = total.astype(jnp.bfloat16)
-    for g in range(out_ref.shape[0]):
-        out_ref[g] = shared
+    out_ref[:, :kept] = columns[:share].astype(jnp.bfloat16)
+    out_ref[:, kept:] = columns[share:, 2 * kept - block :].astype(jnp.bfloat16)
 
 
 def final_kernel(block, totals_ref, out_ref):
-    full = out_ref.shape[1]
-    for g in range(totals_ref.shape[0]):
-        end = min((g + 1) * block, full)
-        out_ref[:, g * block : end] = totals_ref[g, :, : end - g * block].astype(jnp.float32)
+    for g in range(totals_ref.shape[1]):
+        total = totals_ref[0, g].astype(jnp.float32)
+        for t in range(1, totals_ref.shape[0]):
+            total += totals_ref[t, g].astype(jnp.float32)
+        out_ref[:, g * block : (g + 1) * block] = total
 
 
 def shards(enc, enc_dest, enc_group, query, dec_group, out_grad, w_kv):
     peers = lax.axis_size("seq")
     parts = lax.axis_size("part")
-    groups = lax.axis_size("group")
+    line = lax.axis_size("line")
+    groups = line * lax.axis_size("core")
     enc_rows, model = enc.shape
     capacity = 3 * enc_rows // (2 * peers)
     slot_count = peers * capacity
@@ -256,13 +236,10 @@
     norm_factor = 1.0 / math.sqrt(enc_rows * peers * groups * parts)
     block = -(-full // (groups * 8)) * 8
     kept = -(-block // 32) * 16
-    block_lanes = -(-block // LANES) * LANES
     share = model // peers
     chunks = full // LANES
     packed_rows = capacity * chunks
     stride = packed_rows + 8
-
-    enc_all = lax.all_gather(enc, "group", axis=0, tiled=True)
 
     outgoing, placing = pl.pallas_call(
         functools.partial(route_kernel, peers, capacity, stride),
@@ -282,6 +259,8 @@
         ],
         compiler_params=pltpu.CompilerParams(vmem_limit_bytes=64 * MIB),
     )(enc, enc_dest.reshape(1, enc_rows), enc_group.reshape(1, enc_rows), w_kv)
+    mine, outgoing = lax.optimization_barrier((enc, outgoing))
+    passed = [lax.ppermute(mine, "line", [(i, i ^ k) for i in range(line)]) for k in range(1, line)]
     incoming = lax.all_to_all(
         outgoing.reshape(peers, stride, LANES), "seq", split_axis=0, concat_axis=0, tiled=True
     )
@@ -298,7 +277,7 @@
             pltpu.VMEM((slot_count, full), jnp.bfloat16),
             pltpu.VMEM((slot_count, dec_rows), jnp.float32),
         ],
-        compiler_params=pltpu.CompilerParams(vmem_limit_bytes=60 * MIB),
+        compiler_params=pltpu.CompilerParams(vmem_limit_bytes=32 * MIB),
     )(
         incoming.reshape(peers * stride, LANES),
         dec_group.reshape(1, dec_rows),
@@ -306,6 +285,9 @@
         query,
         out_grad,
     )
+    *passed, _ = lax.optimization_barrier((*passed, slot_grad))
+    own = jnp.concatenate([enc] + passed)
+    other = lax.ppermute(own, "core", [(0, 1), (1, 0)])
     returned = lax.all_to_all(
         slot_grad.reshape(peers, packed_rows, LANES), "seq", split_axis=0, concat_axis=0, tiled=True
     )
@@ -319,45 +301,46 @@
     enc_grad = contract(columns[:full], w_kv, ((0,), (1,))).astype(jnp.bfloat16)
 
     blocks = lax.all_to_all(
-        columns.reshape(groups, block, enc_rows), "group", split_axis=0, concat_axis=0, tiled=True
+        columns.reshape(groups, block, enc_rows), ("line", "core"), split_axis=0, concat_axis=0, tiled=True
     )
+    place = jnp.arange(groups, dtype=jnp.int32)
+    order = (lax.axis_index("line") ^ place % line) * 2 + (lax.axis_index("core") ^ place // line)
     tile = pl.pallas_call(
         functools.partial(tile_kernel, block, share, norm_factor),
         out_shape=jax.ShapeDtypeStruct((peers, kept, 2 * share), jnp.bfloat16),
-        in_specs=[pl.BlockSpec(memory_space=pltpu.VMEM), pl.BlockSpec(memory_space=pltpu.HBM)],
+        in_specs=[
+            pl.BlockSpec(memory_space=pltpu.SMEM),
+            pl.BlockSpec(memory_space=pltpu.VMEM),
+            pl.BlockSpec(memory_space=pltpu.HBM),
+            pl.BlockSpec(memory_space=pltpu.HBM),
+        ],
         scratch_shapes=[
             pltpu.VMEM((block, groups * enc_rows), jnp.bfloat16),
             pltpu.VMEM((groups * enc_rows, model), jnp.bfloat16),
             pltpu.VMEM((block, model), jnp.float32),
             pltpu.SemaphoreType.DMA((groups // 2,)),
         ],
-        compiler_params=pltpu.CompilerParams(vmem_limit_bytes=62 * MIB),
-    )(blocks, enc_all)
+        compiler_params=pltpu.CompilerParams(vmem_limit_bytes=32 * MIB),
+    )(order, blocks, own, other)
     tiles = lax.all_to_all(tile, "seq", split_axis=0, concat_axis=0, tiled=True)
     shared = pl.pallas_call(
         functools.partial(sum_kernel, block, share),
-        out_shape=jax.ShapeDtypeStruct((share, block_lanes), jnp.bfloat16),
+        out_shape=jax.ShapeDtypeStruct((share, block), jnp.bfloat16),
         compiler_params=pltpu.CompilerParams(vmem_limit_bytes=32 * MIB),
     )(tiles)
-    shared = lax.all_gather(shared, "part", axis=0, tiled=True).reshape(parts, share, block_lanes)
-    shared = pl.pallas_call(
-        join_kernel,
-        out_shape=jax.ShapeDtypeStruct((groups, share, block_lanes), jnp.bfloat16),
-        compiler_params=pltpu.CompilerParams(vmem_limit_bytes=32 * MIB),
-    )(shared)
-    shared = lax.all_to_all(shared, "group", split_axis=0, concat_axis=0, tiled=True)
+    totals = lax.all_gather(shared, ("part", "line", "core"), axis=0, tiled=True)
     kv_weight_grad = pl.pallas_call(
         functools.partial(final_kernel, block),
         out_shape=jax.ShapeDtypeStruct((share, full), jnp.float32),
         compiler_params=pltpu.CompilerParams(vmem_limit_bytes=32 * MIB),
-    )(shared)
+    )(totals.reshape(parts, groups, share, block))
     return (query_grad, enc_grad, kv_weight_grad)
 
 
 def solution(mesh):
     dp, seq = mesh.devices.shape
-    cut = Mesh(mesh.devices.reshape(PARTS, dp // PARTS, seq), ("part", "group", "seq"))
-    rows = ("part", "group", "seq")
-    in_specs = (P(rows, None), P(rows, None), P(rows), P(rows, None), P(rows), P(rows, None), P())
-    out_specs = (P(rows, None), P(rows, None), P("seq", None))
+    names = ("part", "line", "core", "seq")
+    cut = Mesh(mesh.devices.reshape(dp // (2 * LINE), LINE, 2, seq), names)
+    in_specs = (P(names, None), P(names, None), P(names), P(names, None), P(names), P(names, None), P())
+    out_specs = (P(names, None), P(names, None), P("seq", None))
     return jax.shard_map(shards, mesh=cut, in_specs=in_specs, out_specs=out_specs, check_vma=False)

time: 185 us -> 173 us (0.935)
  blocking collectives: 133 us -> 34.1 us
  starting transfers between devices: 8.44 us -> 56.7 us
  waiting for transfers between devices: 2.31 us -> 49.9 us
  between operations: 14.1 us -> 0.76 us
  local copies, waits for them, and re-layouts: 0.84 us -> 6.88 us
  Pallas kernels: 19 us -> 16.6 us
    all_to_all x4 -> x0, blocking collectives: 115 us -> none  [the longest x1 30.5 us: shards(): lax.all_to_all(columns.reshape(groups, block, enc_rows), 'group', split_a...]
    all_to_all x1 -> x4, waiting for transfers between devices: 1.63 us -> 40.6 us  [the longest x1 18.7 us: shards(): tiles = lax.all_to_all(tile, 'seq', split_axis=0, concat_axis=0, tiled=True)]
    all_to_all x1 -> x4, starting transfers between devices: 8.4 us -> 39.8 us  [the longest x1 15.3 us: shards(): lax.all_to_all(columns.reshape(groups, block, enc_rows), ('line', 'core')...]
    ppermute x0 -> x4, starting transfers between devices: none -> 16.9 us  [the longest x3 11.7 us: shards(): lax.ppermute(mine, 'line', [(i, i ^ k) for i in range(line)])]
    all_gather x1, blocking collectives: 18.2 us -> 34.1 us  [shards(): lax.all_gather(shared, ('part', 'line', 'core'), axis=0, tiled=True)]
    ppermute x0 -> x4, waiting for transfers between devices: none -> 9.34 us  [the longest x3 9.33 us: shards(): lax.ppermute(mine, 'line', [(i, i ^ k) for i in range(line)])]
    unnamed x2 -> x13, local copies, waits for them, and re-layouts: 0.84 us -> 5.8 us
  transfers between devices with their start and end apart: 2 -> 8, of which waited for: 1 -> 4; matrix products, arithmetic and copies ran while one was open for 4% -> 6% of each run, Pallas kernels for 7% -> 3%
where the time goes in v3:
time: 173 us; the launch traced here: 172 us
  starting transfers between devices  56.7 us (33%)
  waiting for transfers between devices  49.9 us (29%)
  blocking collectives  34.1 us (20%)
  Pallas kernels  16.6 us (10%)
  matrix products  7.28 us (4%)
  local copies, waits for them, and re-layouts  6.88 us (4%)
    all_gather x1, blocking collectives, shards(): lax.all_gather(shared, ('part', 'line', 'core'), axis=0, tiled=True)  34.1 us
    all_to_all x1, waiting for transfers between devices, shards(): tiles = lax.all_to_all(tile, 'seq', split_axis=0, concat_axis=0, tiled=True)  18.7 us
    all_to_all x1, starting transfers between devices, shards(): lax.all_to_all(columns.reshape(groups, block, enc_rows), ('line', 'core')...  15.3 us
    all_to_all x1, waiting for transfers between devices, shards(): lax.all_to_all(columns.reshape(groups, block, enc_rows), ('line', 'core')...  14.5 us
    ppermute x3, starting transfers between devices, shards(): lax.ppermute(mine, 'line', [(i, i ^ k) for i in range(line)])  11.7 us
    all_to_all x1, starting transfers between devices, shards(): lax.all_to_all(outgoing.reshape(peers, stride, LANES), 'seq', split_axis=...  10.6 us
    ppermute x3, waiting for transfers between devices, shards(): lax.ppermute(mine, 'line', [(i, i ^ k) for i in range(line)])  9.33 us
    all_to_all x1, waiting for transfers between devices, shards(): lax.all_to_all(outgoing.reshape(peers, stride, LANES), 'seq', split_axis=...  7.38 us
  transfers between devices with their start and end apart: 8, of which 4 were waited for; matrix products, arithmetic and copies ran while one was open for 6% of the time, Pallas kernels for 3%

profile of v3, /device:TPU:1, one launch (start us, length us, event | category | flops | bytes accessed | tf_op | source)
XLA Modules:
  0.0 172.2 jit_solution(4710371039247455890)
XLA Ops:
  0.6 5.7 %shard_map.94 = (bf16[3328,128]{1,0:T(8,128)(2,1)}, bf16[128,192]{1,0:T(8,128)(2,1)}) custom-call(bf16[128,2048]{1,0:T(8,128)(2,1)} %enc_hbm.1, s32[1,128]{1,0:T(1,128)} %bitcast.16, s32[1,128]{1,0:T(1,128)} %bitcast.17, bf16[2048,2048]{1,0:T(8,128)(2,1)} %w_hbm.1), custom_call_target="tpu_custom_call" | custom-call | tf_op jit(solution)/shard_map/pallas_call | solution.py:244
  6.4 10.6 %all-to-all-start = ((bf16[32,104,128]{2,1,0:T(8,128)(2,1)}), bf16[32,104,128]{2,1,0:T(8,128)(2,1)S(1)}, u32[]{:S(2)}, u32[]{:S(2)}) async-start(bf16[32,104,128]{2,1,0:T(8,128)(2,1)} %bitcast.15), calls=%async_computation | async-start | bytes 1703936 | tf_op jit(solution)/shard_map/all_to_all | solution.py:264
  17.0 4.0 %collective-permute-start = (bf16[128,2048]{1,0:T(8,128)(2,1)}, bf16[128,2048]{1,0:T(8,128)(2,1)}, u32[]{:S(2)}, u32[]{:S(2)}) collective-permute-start(bf16[128,2048]{1,0:T(8,128)(2,1)} %enc_hbm.1), channel_id=1, source_target_pairs={{0,64},{64,0},{128,192},{192,128},{1,65},{65,1},{129,193},{193,129... | collective-permute-start | bytes 1572872 | tf_op jit(solution)/shard_map/ppermute | solution.py:263
  21.0 5.8 %collective-permute-start.1 = (bf16[128,2048]{1,0:T(8,128)(2,1)}, bf16[128,2048]{1,0:T(8,128)(2,1)}, u32[]{:S(2)}, u32[]{:S(2)}) collective-permute-start(bf16[128,2048]{1,0:T(8,128)(2,1)} %enc_hbm.1), channel_id=1, source_target_pairs={{0,128},{64,192},{128,0},{192,64},{1,129},{65,193},{129,1},{193,65... | collective-permute-start | bytes 1572872 | tf_op jit(solution)/shard_map/ppermute | solution.py:263
  26.9 1.9 %collective-permute-start.2 = (bf16[128,2048]{1,0:T(8,128)(2,1)}, bf16[128,2048]{1,0:T(8,128)(2,1)}, u32[]{:S(2)}, u32[]{:S(2)}) collective-permute-start(bf16[128,2048]{1,0:T(8,128)(2,1)} %enc_hbm.1), channel_id=1, source_target_pairs={{0,192},{64,128},{128,64},{192,0},{1,193},{65,129},{129,65},{193,1... | collective-permute-start | bytes 1572872 | tf_op jit(solution)/shard_map/ppermute | solution.py:263
  28.8 7.4 %all-to-all-done = bf16[32,104,128]{2,1,0:T(8,128)(2,1)S(1)} async-done(((bf16[32,104,128]{2,1,0:T(8,128)(2,1)}), bf16[32,104,128]{2,1,0:T(8,128)(2,1)S(1)}, u32[]{:S(2)}, u32[]{:S(2)}) %all-to-all-start) | async-done | bytes 852000 | tf_op jit(solution)/shard_map/all_to_all | solution.py:264
  36.2 1.0 copy-done
  37.2 1.0 copy-done.1
  39.8 4.2 %shard_map.95 = (bf16[256,1024]{1,0:T(8,128)(2,1)}, bf16[3072,128]{1,0:T(8,128)(2,1)}, bf16[128,192]{1,0:T(8,128)(2,1)S(1)}) custom-call(bf16[3328,128]{1,0:T(8,128)(2,1)S(1)} %bitcast.11, s32[1,256]{1,0:T(1,128)S(1)} %bitcast.14, bf16[128,192]{1,0:T(8,128)(2,1)S(1)} %copy-done.2, bf16[256,1024]{1,0:T(8,128)(2,1)S(1)} %copy-done, bf16[256,1024]{1,0:T(8,128)(2,1)S(1)} %copy-done.1), custom_call_target="tpu_custom_call" | custom-call | tf_op jit(solution)/shard_map/pallas_call | solution.py:268
  44.0 7.3 %all-to-all-start.1 = ((bf16[32,96,128]{2,1,0:T(8,128)(2,1)}), bf16[32,96,128]{2,1,0:T(8,128)(2,1)S(1)}, u32[]{:S(2)}, u32[]{:S(2)}) async-start(bf16[32,96,128]{2,1,0:T(8,128)(2,1)} %bitcast.5), calls=%async_computation.1 | async-start | bytes 1572864 | tf_op jit(solution)/shard_map/all_to_all | solution.py:291
  51.4 9.3 %collective-permute-done.1 = bf16[128,2048]{1,0:T(8,128)(2,1)} collective-permute-done((bf16[128,2048]{1,0:T(8,128)(2,1)}, bf16[128,2048]{1,0:T(8,128)(2,1)}, u32[]{:S(2)}, u32[]{:S(2)}) %collective-permute-start.1) | collective-permute-done | bytes 524320 | tf_op jit(solution)/shard_map/ppermute | solution.py:263
  60.7 1.1 constant_dynamic-update-slice_fusion.2
  61.8 1.1 constant_dynamic-update-slice_fusion.1
  62.9 1.1 constant_dynamic-update-slice_fusion.own_hbm
  64.0 5.2 %collective-permute-start.3 = (bf16[512,2048]{1,0:T(8,128)(2,1)S(1)}, bf16[512,2048]{1,0:T(8,128)(2,1)}, u32[]{:S(2)}, u32[]{:S(2)}) collective-permute-start(bf16[512,2048]{1,0:T(8,128)(2,1)S(1)} %constant_dynamic-update-slice_fusion.own_hbm), channel_id=1, source_target_pairs={{0,32},{32,0},{1,33},{33,1},{2,34},{34,2},{3,35},{35,3},{4,36},{36... | collective-permute-start | bytes 6291464 | tf_op jit(solution)/shard_map/ppermute | solution.py:290
  69.1 1.7 shard_map.96
  70.8 15.3 %all-to-all-start.2 = ((bf16[8,256,128]{2,1,0:T(8,128)(2,1)}), bf16[8,256,128]{2,1,0:T(8,128)(2,1)S(1)}, u32[]{:S(2)}, u32[]{:S(2)}) async-start(bf16[8,256,128]{2,1,0:T(8,128)(2,1)} %bitcast.7), calls=%async_computation.2 | async-start | bytes 1048576 | tf_op jit(solution)/shard_map/all_to_all | solution.py:303
  86.1 14.5 %all-to-all-done.2.blocks_ref = bf16[8,256,128]{2,1,0:T(8,128)(2,1)S(1)} async-done(((bf16[8,256,128]{2,1,0:T(8,128)(2,1)}), bf16[8,256,128]{2,1,0:T(8,128)(2,1)S(1)}, u32[]{:S(2)}, u32[]{:S(2)}) %all-to-all-start.2) | async-done | bytes 524320 | tf_op jit(solution)/shard_map/all_to_all | solution.py:303
  100.6 3.8 %shard_map.97 = bf16[32,128,128]{2,1,0:T(8,128)(2,1)} custom-call(s32[8]{0:T(128)S(1)} %fusion.2.order_ref, bf16[8,256,128]{2,1,0:T(8,128)(2,1)S(1)} %all-to-all-done.2.blocks_ref, bf16[512,2048]{1,0:T(8,128)(2,1)S(1)} %constant_dynamic-update-slice_fusion.own_hbm, bf16[512,2048]{1,0:T(8,128)(2,1)} %collective-permute-done.3.other_hbm), custom_call_target="tpu_custom_call" | custom-call | tf_op jit(solution)/shard_map/pallas_call | solution.py:308
  104.5 6.6 %all-to-all-start.3 = ((bf16[32,128,128]{2,1,0:T(8,128)(2,1)}), bf16[32,128,128]{2,1,0:T(8,128)(2,1)S(1)}, u32[]{:S(2)}, u32[]{:S(2)}) async-start(bf16[32,128,128]{2,1,0:T(8,128)(2,1)} %shard_map.97), calls=%async_computation.3 | async-start | bytes 2097152 | tf_op jit(solution)/shard_map/all_to_all | solution.py:325
  111.1 7.3 %convolution_convert_fusion = bf16[128,2048]{1,0:T(8,128)(2,1)} fusion(bf16[2048,128]{1,0:T(8,128)(2,1)} %shard_map.96, bf16[2048,2048]{1,0:T(8,128)(2,1)} %w_hbm.1), kind=kOutput, calls=%fused_computation | convolution fusion | flops 1074003968 | bytes 9437184 | tf_op jit(solution)/shard_map/dot_general | solution.py:20
  118.4 18.7 %all-to-all-done.3.parts_ref = bf16[32,128,128]{2,1,0:T(8,128)(2,1)S(1)} async-done(((bf16[32,128,128]{2,1,0:T(8,128)(2,1)}), bf16[32,128,128]{2,1,0:T(8,128)(2,1)S(1)}, u32[]{:S(2)}, u32[]{:S(2)}) %all-to-all-start.3) | async-done | bytes 1048608 | tf_op jit(solution)/shard_map/all_to_all | solution.py:325
  137.3 34.1 %all_gather.3 = bf16[1536,256]{1,0:T(8,128)(2,1)S(1)} all-gather(bf16[64,256]{1,0:T(8,128)(2,1)S(1)} %shard_map.98), channel_id=1, replica_groups=mesh['part'=3,'line'=4,'core'=2,'seq'=32] {'part','line','core'}, dimensions={0}, use_global_device_ids=true | all-gather | bytes 819200 | tf_op jit(solution)/shard_map/all_gather | solution.py:331
  171.4 0.9 shard_map.99
  (15 shorter events, 1.8 us)
Async XLA Ops:
  6.4 45.0 %copy-start.4 = (bf16[128,2048]{1,0:T(8,128)(2,1)S(1)}, bf16[128,2048]{1,0:T(8,128)(2,1)}, u32[]{:S(2)}) copy-start(bf16[128,2048]{1,0:T(8,128)(2,1)} %enc_hbm.1) | copy-start | bytes 1572868
  6.4 29.8 %all-to-all-start = ((bf16[32,104,128]{2,1,0:T(8,128)(2,1)}), bf16[32,104,128]{2,1,0:T(8,128)(2,1)S(1)}, u32[]{:S(2)}, u32[]{:S(2)}) async-start(bf16[32,104,128]{2,1,0:T(8,128)(2,1)} %bitcast.15), calls=%async_computation | async-start | bytes 1703936 | tf_op jit(solution)/shard_map/all_to_all | solution.py:264
  17.0 34.4 %collective-permute-start = (bf16[128,2048]{1,0:T(8,128)(2,1)}, bf16[128,2048]{1,0:T(8,128)(2,1)}, u32[]{:S(2)}, u32[]{:S(2)}) collective-permute-start(bf16[128,2048]{1,0:T(8,128)(2,1)} %enc_hbm.1), channel_id=1, source_target_pairs={{0,64},{64,0},{128,192},{192,128},{1,65},{65,1},{129,193},{193,129... | collective-permute-start | bytes 1572872 | tf_op jit(solution)/shard_map/ppermute | solution.py:263
  21.0 39.7 %collective-permute-start.1 = (bf16[128,2048]{1,0:T(8,128)(2,1)}, bf16[128,2048]{1,0:T(8,128)(2,1)}, u32[]{:S(2)}, u32[]{:S(2)}) collective-permute-start(bf16[128,2048]{1,0:T(8,128)(2,1)} %enc_hbm.1), channel_id=1, source_target_pairs={{0,128},{64,192},{128,0},{192,64},{1,129},{65,193},{129,1},{193,65... | collective-permute-start | bytes 1572872 | tf_op jit(solution)/shard_map/ppermute | solution.py:263
  26.9 33.9 %collective-permute-start.2 = (bf16[128,2048]{1,0:T(8,128)(2,1)}, bf16[128,2048]{1,0:T(8,128)(2,1)}, u32[]{:S(2)}, u32[]{:S(2)}) collective-permute-start(bf16[128,2048]{1,0:T(8,128)(2,1)} %enc_hbm.1), channel_id=1, source_target_pairs={{0,192},{64,128},{128,64},{192,0},{1,193},{65,129},{129,65},{193,1... | collective-permute-start | bytes 1572872 | tf_op jit(solution)/shard_map/ppermute | solution.py:263
  36.2 1.0 copy-start
  37.2 1.0 copy-start.1
  38.3 0.8 copy-start.2
  39.1 0.7 copy-start.3
  44.0 25.1 %all-to-all-start.1 = ((bf16[32,96,128]{2,1,0:T(8,128)(2,1)}), bf16[32,96,128]{2,1,0:T(8,128)(2,1)S(1)}, u32[]{:S(2)}, u32[]{:S(2)}) async-start(bf16[32,96,128]{2,1,0:T(8,128)(2,1)} %bitcast.5), calls=%async_computation.1 | async-start | bytes 1572864 | tf_op jit(solution)/shard_map/all_to_all | solution.py:291
  64.0 22.2 %collective-permute-start.3 = (bf16[512,2048]{1,0:T(8,128)(2,1)S(1)}, bf16[512,2048]{1,0:T(8,128)(2,1)}, u32[]{:S(2)}, u32[]{:S(2)}) collective-permute-start(bf16[512,2048]{1,0:T(8,128)(2,1)S(1)} %constant_dynamic-update-slice_fusion.own_hbm), channel_id=1, source_target_pairs={{0,32},{32,0},{1,33},{33,1},{2,34},{34,2},{3,35},{35,3},{4,36},{36... | collective-permute-start | bytes 6291464 | tf_op jit(solution)/shard_map/ppermute | solution.py:290
  70.8 29.8 %all-to-all-start.2 = ((bf16[8,256,128]{2,1,0:T(8,128)(2,1)}), bf16[8,256,128]{2,1,0:T(8,128)(2,1)S(1)}, u32[]{:S(2)}, u32[]{:S(2)}) async-start(bf16[8,256,128]{2,1,0:T(8,128)(2,1)} %bitcast.7), calls=%async_computation.2 | async-start | bytes 1048576 | tf_op jit(solution)/shard_map/all_to_all | solution.py:303
  104.5 32.6 %all-to-all-start.3 = ((bf16[32,128,128]{2,1,0:T(8,128)(2,1)}), bf16[32,128,128]{2,1,0:T(8,128)(2,1)S(1)}, u32[]{:S(2)}, u32[]{:S(2)}) async-start(bf16[32,128,128]{2,1,0:T(8,128)(2,1)} %shard_map.97), calls=%async_computation.3 | async-start | bytes 2097152 | tf_op jit(solution)/shard_map/all_to_all | solution.py:325

commit v4 on v3

--- a/solution.py
+++ b/solution.py
@@ -104,18 +104,40 @@
     out_ref[...] = wide[...].astype(jnp.bfloat16)
 
 
+def stage_kernel(count, *refs):
+    sources, targets, sems = refs[:count], refs[-count - 1 : -1], refs[-1]
+    copies = [
+        pltpu.make_async_copy(source, target, sems.at[k])
+        for k, (source, target) in enumerate(zip(sources, targets))
+    ]
+    for copy in copies:
+        copy.start()
+    for copy in copies:
+        copy.wait()
+
+
+def stage(arrays, after):
+    count = len(arrays)
+    return pl.pallas_call(
+        functools.partial(stage_kernel, count),
+        out_shape=tuple(jax.ShapeDtypeStruct(a.shape, a.dtype) for a in arrays),
+        in_specs=[pl.BlockSpec(memory_space=pltpu.HBM)] * count + [pl.BlockSpec(memory_space=pl.ANY)],
+        out_specs=tuple(pl.BlockSpec(memory_space=pltpu.VMEM) for a in arrays),
+        scratch_shapes=[pltpu.SemaphoreType.DMA((count,))],
+        compiler_params=pltpu.CompilerParams(vmem_limit_bytes=32 * MIB),
+    )(*arrays, after)
+
+
 def attention_kernel(
     peers,
     capacity,
     stride,
     incoming_ref,
     group_ref,
-    placing_ref,
     query_ref,
     grad_ref,
     query_grad_ref,
     out_ref,
-    placing_out_ref,
     wide,
     received,
     bias,
@@ -124,7 +146,6 @@
     chunks = model // LANES
     width = HEADS * HEAD_DIM
     scale = 1.0 / math.sqrt(HEAD_DIM)
-    placing_out_ref[...] = placing_ref[...]
     wide[...] = incoming_ref[...].astype(jnp.float32)
     for r in range(capacity):
         for c in range(chunks):
@@ -260,17 +281,19 @@
         compiler_params=pltpu.CompilerParams(vmem_limit_bytes=64 * MIB),
     )(enc, enc_dest.reshape(1, enc_rows), enc_group.reshape(1, enc_rows), w_kv)
     mine, outgoing = lax.optimization_barrier((enc, outgoing))
-    passed = [lax.ppermute(mine, "line", [(i, i ^ k) for i in range(line)]) for k in range(1, line)]
+    passed = [lax.ppermute(mine, "line", [(i, i ^ k) for i in range(line)]) for k in range(line - 1, 0, -1)]
     incoming = lax.all_to_all(
         outgoing.reshape(peers, stride, LANES), "seq", split_axis=0, concat_axis=0, tiled=True
     )
 
-    query_grad, slot_grad, placing = pl.pallas_call(
+    query_near, grad_near, group_near, placing_near = stage(
+        (query, out_grad, dec_group.reshape(1, dec_rows), placing), placing
+    )
+    query_grad, slot_grad = pl.pallas_call(
         functools.partial(attention_kernel, peers, capacity, stride),
         out_shape=(
             jax.ShapeDtypeStruct((dec_rows, width), jnp.bfloat16),
             jax.ShapeDtypeStruct((peers * packed_rows, LANES), jnp.bfloat16),
-            jax.ShapeDtypeStruct((enc_rows, slot_count), jnp.bfloat16),
         ),
         scratch_shapes=[
             pltpu.VMEM((peers * stride, LANES), jnp.float32),
@@ -278,15 +301,9 @@
             pltpu.VMEM((slot_count, dec_rows), jnp.float32),
         ],
         compiler_params=pltpu.CompilerParams(vmem_limit_bytes=32 * MIB),
-    )(
-        incoming.reshape(peers * stride, LANES),
-        dec_group.reshape(1, dec_rows),
-        placing,
-        query,
-        out_grad,
-    )
+    )(incoming.reshape(peers * stride, LANES), group_near, query_near, grad_near)
     *passed, _ = lax.optimization_barrier((*passed, slot_grad))
-    own = jnp.concatenate([enc] + passed)
+    own = jnp.concatenate([enc] + passed[::-1])
     other = lax.ppermute(own, "core", [(0, 1), (1, 0)])
     returned = lax.all_to_all(
         slot_grad.reshape(peers, packed_rows, LANES), "seq", split_axis=0, concat_axis=0, tiled=True
@@ -297,7 +314,7 @@
         out_shape=jax.ShapeDtypeStruct((groups * block, enc_rows), jnp.bfloat16),
         scratch_shapes=[pltpu.VMEM((peers * packed_rows, LANES), jnp.float32)],
         compiler_params=pltpu.CompilerParams(vmem_limit_bytes=32 * MIB),
-    )(returned.reshape(peers * packed_rows, LANES), placing)
+    )(returned.reshape(peers * packed_rows, LANES), placing_near)
     enc_grad = contract(columns[:full], w_kv, ((0,), (1,))).astype(jnp.bfloat16)
 
     blocks = lax.all_to_all(

time: 173 us -> 171 us (0.988)
  starting transfers between devices: 56.7 us -> 46.3 us
  waiting for transfers between devices: 49.9 us -> 57.2 us
    ppermute x3, waiting for transfers between devices: 9.33 us -> 20.4 us  [shards(): lax.ppermute(mine, 'line', [(i, i ^ k) for i in range(line)])]
    all_to_all x1, starting transfers between devices: 15.3 us -> 5.93 us  [shards(): lax.all_to_all(columns.reshape(groups, block, enc_rows), ('line', 'core')...]
    all_to_all x1, waiting for transfers between devices: 7.38 us -> 3.57 us  [shards(): lax.all_to_all(outgoing.reshape(peers, stride, LANES), 'seq', split_axis=...]
  transfers between devices with their start and end apart: 8 -> 8, of which waited for: 4 -> 4; matrix products, arithmetic and copies ran while one was open for 6% -> 6% of each run, Pallas kernels for 3% -> 4%
where the time goes in v4:
time: 171 us; the launch traced here: 170 us
  waiting for transfers between devices  57.2 us (33%)
  starting transfers between devices  46.3 us (27%)
  blocking collectives  34.7 us (20%)
  Pallas kernels  16.8 us (10%)
  matrix products  7.28 us (4%)
  local copies, waits for them, and re-layouts  6.87 us (4%)
    all_gather x1, blocking collectives, shards(): lax.all_gather(shared, ('part', 'line', 'core'), axis=0, tiled=True)  34.7 us
    ppermute x3, waiting for transfers between devices, shards(): lax.ppermute(mine, 'line', [(i, i ^ k) for i in range(line)])  20.4 us
    all_to_all x1, waiting for transfers between devices, shards(): tiles = lax.all_to_all(tile, 'seq', split_axis=0, concat_axis=0, tiled=True)  18.7 us
    all_to_all x1, waiting for transfers between devices, shards(): lax.all_to_all(columns.reshape(groups, block, enc_rows), ('line', 'core')...  14.5 us
    ppermute x3, starting transfers between devices, shards(): lax.ppermute(mine, 'line', [(i, i ^ k) for i in range(line)])  11.7 us
    all_to_all x1, starting transfers between devices, shards(): lax.all_to_all(outgoing.reshape(peers, stride, LANES), 'seq', split_axis=...  10.5 us
    all_to_all x1, starting transfers between devices, shards(): tiles = lax.all_to_all(tile, 'seq', split_axis=0, concat_axis=0, tiled=True)  7.33 us
    all_to_all x1, starting transfers between devices, shards(): lax.all_to_all(slot_grad.reshape(peers, packed_rows, LANES), 'seq', split...  7.32 us
  transfers between devices with their start and end apart: 8, of which 4 were waited for; matrix products, arithmetic and copies ran while one was open for 6% of the time, Pallas kernels for 4%

profile of v4, /device:TPU:1, one launch (start us, length us, event | category | flops | bytes accessed | tf_op | source)
XLA Modules:
  0.0 169.8 jit_solution(17562430708929115221)
XLA Ops:
  0.6 5.7 %shard_map.94 = (bf16[3328,128]{1,0:T(8,128)(2,1)}, bf16[128,192]{1,0:T(8,128)(2,1)}) custom-call(bf16[128,2048]{1,0:T(8,128)(2,1)} %enc_hbm.1, s32[1,128]{1,0:T(1,128)} %bitcast.16, s32[1,128]{1,0:T(1,128)} %bitcast.17, bf16[2048,2048]{1,0:T(8,128)(2,1)} %w_hbm.1), custom_call_target="tpu_custom_call" | custom-call | tf_op jit(solution)/shard_map/pallas_call | solution.py:265
  6.4 10.5 %all-to-all-start = ((bf16[32,104,128]{2,1,0:T(8,128)(2,1)}), bf16[32,104,128]{2,1,0:T(8,128)(2,1)S(1)}, u32[]{:S(2)}, u32[]{:S(2)}) async-start(bf16[32,104,128]{2,1,0:T(8,128)(2,1)} %bitcast.15), calls=%async_computation | async-start | bytes 1703936 | tf_op jit(solution)/shard_map/all_to_all | solution.py:285
  16.9 7.6 %collective-permute-start = (bf16[128,2048]{1,0:T(8,128)(2,1)}, bf16[128,2048]{1,0:T(8,128)(2,1)}, u32[]{:S(2)}, u32[]{:S(2)}) collective-permute-start(bf16[128,2048]{1,0:T(8,128)(2,1)} %enc_hbm.1), channel_id=1, source_target_pairs={{0,192},{64,128},{128,64},{192,0},{1,193},{65,129},{129,65},{193,1... | collective-permute-start | bytes 1572872 | tf_op jit(solution)/shard_map/ppermute | solution.py:284
  24.5 1.9 %collective-permute-start.1 = (bf16[128,2048]{1,0:T(8,128)(2,1)}, bf16[128,2048]{1,0:T(8,128)(2,1)}, u32[]{:S(2)}, u32[]{:S(2)}) collective-permute-start(bf16[128,2048]{1,0:T(8,128)(2,1)} %enc_hbm.1), channel_id=1, source_target_pairs={{0,128},{64,192},{128,0},{192,64},{1,129},{65,193},{129,1},{193,65... | collective-permute-start | bytes 1572872 | tf_op jit(solution)/shard_map/ppermute | solution.py:284
  26.4 2.2 %collective-permute-start.2 = (bf16[128,2048]{1,0:T(8,128)(2,1)}, bf16[128,2048]{1,0:T(8,128)(2,1)}, u32[]{:S(2)}, u32[]{:S(2)}) collective-permute-start(bf16[128,2048]{1,0:T(8,128)(2,1)} %enc_hbm.1), channel_id=1, source_target_pairs={{0,64},{64,0},{128,192},{192,128},{1,65},{65,1},{129,193},{193,129... | collective-permute-start | bytes 1572872 | tf_op jit(solution)/shard_map/ppermute | solution.py:284
  28.7 1.0 copy-done
  29.7 1.0 copy-done.1
  32.5 3.6 %all-to-all-done = bf16[32,104,128]{2,1,0:T(8,128)(2,1)S(1)} async-done(((bf16[32,104,128]{2,1,0:T(8,128)(2,1)}), bf16[32,104,128]{2,1,0:T(8,128)(2,1)S(1)}, u32[]{:S(2)}, u32[]{:S(2)}) %all-to-all-start) | async-done | bytes 852000 | tf_op jit(solution)/shard_map/all_to_all | solution.py:285
  36.0 4.2 %shard_map.96 = (bf16[256,1024]{1,0:T(8,128)(2,1)}, bf16[3072,128]{1,0:T(8,128)(2,1)}) custom-call(bf16[3328,128]{1,0:T(8,128)(2,1)S(1)} %bitcast.11, s32[1,256]{1,0:T(1,128)S(1)} %get-tuple-element.19.group_ref, bf16[256,1024]{1,0:T(8,128)(2,1)S(1)} %get-tuple-element.20.query_ref, bf16[256,1024]{1,0:T(8,128)(2,1)S(1)} %get-tuple-element.21.grad_ref), custom_call_target="tpu_custom_call" | custom-call | tf_op jit(solution)/shard_map/pallas_call | solution.py:292
  40.2 7.3 %all-to-all-start.1 = ((bf16[32,96,128]{2,1,0:T(8,128)(2,1)}), bf16[32,96,128]{2,1,0:T(8,128)(2,1)S(1)}, u32[]{:S(2)}, u32[]{:S(2)}) async-start(bf16[32,96,128]{2,1,0:T(8,128)(2,1)} %bitcast.5), calls=%async_computation.1 | async-start | bytes 1572864 | tf_op jit(solution)/shard_map/all_to_all | solution.py:308
  47.6 20.4 %collective-permute-done.1 = bf16[128,2048]{1,0:T(8,128)(2,1)} collective-permute-done((bf16[128,2048]{1,0:T(8,128)(2,1)}, bf16[128,2048]{1,0:T(8,128)(2,1)}, u32[]{:S(2)}, u32[]{:S(2)}) %collective-permute-start.1) | collective-permute-done | bytes 524320 | tf_op jit(solution)/shard_map/ppermute | solution.py:284
  68.0 1.1 constant_dynamic-update-slice_fusion.2
  69.1 1.1 constant_dynamic-update-slice_fusion.1
  70.2 1.1 constant_dynamic-update-slice_fusion.own_hbm
  71.3 3.5 %collective-permute-start.3 = (bf16[512,2048]{1,0:T(8,128)(2,1)S(1)}, bf16[512,2048]{1,0:T(8,128)(2,1)}, u32[]{:S(2)}, u32[]{:S(2)}) collective-permute-start(bf16[512,2048]{1,0:T(8,128)(2,1)S(1)} %constant_dynamic-update-slice_fusion.own_hbm), channel_id=1, source_target_pairs={{0,32},{32,0},{1,33},{33,1},{2,34},{34,2},{3,35},{35,3},{4,36},{36... | collective-permute-start | bytes 6291464 | tf_op jit(solution)/shard_map/ppermute | solution.py:307
  74.8 1.7 shard_map.97
  76.4 5.9 %all-to-all-start.2 = ((bf16[8,256,128]{2,1,0:T(8,128)(2,1)}), bf16[8,256,128]{2,1,0:T(8,128)(2,1)S(1)}, u32[]{:S(2)}, u32[]{:S(2)}) async-start(bf16[8,256,128]{2,1,0:T(8,128)(2,1)} %bitcast.7), calls=%async_computation.2 | async-start | bytes 1048576 | tf_op jit(solution)/shard_map/all_to_all | solution.py:320
  82.4 14.5 %all-to-all-done.2.blocks_ref = bf16[8,256,128]{2,1,0:T(8,128)(2,1)S(1)} async-done(((bf16[8,256,128]{2,1,0:T(8,128)(2,1)}), bf16[8,256,128]{2,1,0:T(8,128)(2,1)S(1)}, u32[]{:S(2)}, u32[]{:S(2)}) %all-to-all-start.2) | async-done | bytes 524320 | tf_op jit(solution)/shard_map/all_to_all | solution.py:320
  96.9 3.8 %shard_map.98 = bf16[32,128,128]{2,1,0:T(8,128)(2,1)} custom-call(s32[8]{0:T(128)S(1)} %fusion.2.order_ref, bf16[8,256,128]{2,1,0:T(8,128)(2,1)S(1)} %all-to-all-done.2.blocks_ref, bf16[512,2048]{1,0:T(8,128)(2,1)S(1)} %constant_dynamic-update-slice_fusion.own_hbm, bf16[512,2048]{1,0:T(8,128)(2,1)} %collective-permute-done.3.other_hbm), custom_call_target="tpu_custom_call" | custom-call | tf_op jit(solution)/shard_map/pallas_call | solution.py:325
  100.7 7.3 %all-to-all-start.3 = ((bf16[32,128,128]{2,1,0:T(8,128)(2,1)}), bf16[32,128,128]{2,1,0:T(8,128)(2,1)S(1)}, u32[]{:S(2)}, u32[]{:S(2)}) async-start(bf16[32,128,128]{2,1,0:T(8,128)(2,1)} %shard_map.98), calls=%async_computation.3 | async-start | bytes 2097152 | tf_op jit(solution)/shard_map/all_to_all | solution.py:342
  108.1 7.3 %convolution_convert_fusion = bf16[128,2048]{1,0:T(8,128)(2,1)} fusion(bf16[2048,128]{1,0:T(8,128)(2,1)} %shard_map.97, bf16[2048,2048]{1,0:T(8,128)(2,1)} %w_hbm.1), kind=kOutput, calls=%fused_computation | convolution fusion | flops 1074003968 | bytes 9437184 | tf_op jit(solution)/shard_map/dot_general | solution.py:20
  115.3 18.7 %all-to-all-done.3.parts_ref = bf16[32,128,128]{2,1,0:T(8,128)(2,1)S(1)} async-done(((bf16[32,128,128]{2,1,0:T(8,128)(2,1)}), bf16[32,128,128]{2,1,0:T(8,128)(2,1)S(1)}, u32[]{:S(2)}, u32[]{:S(2)}) %all-to-all-start.3) | async-done | bytes 1048608 | tf_op jit(solution)/shard_map/all_to_all | solution.py:342
  134.3 34.7 %all_gather.3 = bf16[1536,256]{1,0:T(8,128)(2,1)S(1)} all-gather(bf16[64,256]{1,0:T(8,128)(2,1)S(1)} %shard_map.99), channel_id=1, replica_groups=mesh['part'=3,'line'=4,'core'=2,'seq'=32] {'part','line','core'}, dimensions={0}, use_global_device_ids=true | all-gather | bytes 819200 | tf_op jit(solution)/shard_map/all_gather | solution.py:348
  169.0 0.9 shard_map.100
  (16 shorter events, 2.0 us)
Async XLA Ops:
  6.4 29.7 %all-to-all-start = ((bf16[32,104,128]{2,1,0:T(8,128)(2,1)}), bf16[32,104,128]{2,1,0:T(8,128)(2,1)S(1)}, u32[]{:S(2)}, u32[]{:S(2)}) async-start(bf16[32,104,128]{2,1,0:T(8,128)(2,1)} %bitcast.15), calls=%async_computation | async-start | bytes 1703936 | tf_op jit(solution)/shard_map/all_to_all | solution.py:285
  16.9 30.8 %collective-permute-start = (bf16[128,2048]{1,0:T(8,128)(2,1)}, bf16[128,2048]{1,0:T(8,128)(2,1)}, u32[]{:S(2)}, u32[]{:S(2)}) collective-permute-start(bf16[128,2048]{1,0:T(8,128)(2,1)} %enc_hbm.1), channel_id=1, source_target_pairs={{0,192},{64,128},{128,64},{192,0},{1,193},{65,129},{129,65},{193,1... | collective-permute-start | bytes 1572872 | tf_op jit(solution)/shard_map/ppermute | solution.py:284
  24.5 43.5 %collective-permute-start.1 = (bf16[128,2048]{1,0:T(8,128)(2,1)}, bf16[128,2048]{1,0:T(8,128)(2,1)}, u32[]{:S(2)}, u32[]{:S(2)}) collective-permute-start(bf16[128,2048]{1,0:T(8,128)(2,1)} %enc_hbm.1), channel_id=1, source_target_pairs={{0,128},{64,192},{128,0},{192,64},{1,129},{65,193},{129,1},{193,65... | collective-permute-start | bytes 1572872 | tf_op jit(solution)/shard_map/ppermute | solution.py:284
  26.4 41.6 %collective-permute-start.2 = (bf16[128,2048]{1,0:T(8,128)(2,1)}, bf16[128,2048]{1,0:T(8,128)(2,1)}, u32[]{:S(2)}, u32[]{:S(2)}) collective-permute-start(bf16[128,2048]{1,0:T(8,128)(2,1)} %enc_hbm.1), channel_id=1, source_target_pairs={{0,64},{64,0},{128,192},{192,128},{1,65},{65,1},{129,193},{193,129... | collective-permute-start | bytes 1572872 | tf_op jit(solution)/shard_map/ppermute | solution.py:284
  28.6 1.0 copy-start
  29.7 1.0 copy-start.1
  30.7 0.8 copy-start.2
  31.6 0.7 copy-start.3
  32.2 15.3 %copy-start.4 = (bf16[128,2048]{1,0:T(8,128)(2,1)S(1)}, bf16[128,2048]{1,0:T(8,128)(2,1)}, u32[]{:S(2)}) copy-start(bf16[128,2048]{1,0:T(8,128)(2,1)} %enc_hbm.1) | copy-start | bytes 1572868
  40.2 34.5 %all-to-all-start.1 = ((bf16[32,96,128]{2,1,0:T(8,128)(2,1)}), bf16[32,96,128]{2,1,0:T(8,128)(2,1)S(1)}, u32[]{:S(2)}, u32[]{:S(2)}) async-start(bf16[32,96,128]{2,1,0:T(8,128)(2,1)} %bitcast.5), calls=%async_computation.1 | async-start | bytes 1572864 | tf_op jit(solution)/shard_map/all_to_all | solution.py:308
  71.3 11.1 %collective-permute-start.3 = (bf16[512,2048]{1,0:T(8,128)(2,1)S(1)}, bf16[512,2048]{1,0:T(8,128)(2,1)}, u32[]{:S(2)}, u32[]{:S(2)}) collective-permute-start(bf16[512,2048]{1,0:T(8,128)(2,1)S(1)} %constant_dynamic-update-slice_fusion.own_hbm), channel_id=1, source_target_pairs={{0,32},{32,0},{1,33},{33,1},{2,34},{34,2},{3,35},{35,3},{4,36},{36... | collective-permute-start | bytes 6291464 | tf_op jit(solution)/shard_map/ppermute | solution.py:307
  76.4 20.4 %all-to-all-start.2 = ((bf16[8,256,128]{2,1,0:T(8,128)(2,1)}), bf16[8,256,128]{2,1,0:T(8,128)(2,1)S(1)}, u32[]{:S(2)}, u32[]{:S(2)}) async-start(bf16[8,256,128]{2,1,0:T(8,128)(2,1)} %bitcast.7), calls=%async_computation.2 | async-start | bytes 1048576 | tf_op jit(solution)/shard_map/all_to_all | solution.py:320
  100.7 33.3 %all-to-all-start.3 = ((bf16[32,128,128]{2,1,0:T(8,128)(2,1)}), bf16[32,128,128]{2,1,0:T(8,128)(2,1)S(1)}, u32[]{:S(2)}, u32[]{:S(2)}) async-start(bf16[32,128,128]{2,1,0:T(8,128)(2,1)} %shard_map.98), calls=%async_computation.3 | async-start | bytes 2097152 | tf_op jit(solution)/shard_map/all_to_all | solution.py:342

commit v5 on v4

--- a/solution.py
+++ b/solution.py
@@ -320,6 +320,7 @@
     blocks = lax.all_to_all(
         columns.reshape(groups, block, enc_rows), ("line", "core"), split_axis=0, concat_axis=0, tiled=True
     )
+    blocks, enc_grad = lax.optimization_barrier((blocks, enc_grad))
     place = jnp.arange(groups, dtype=jnp.int32)
     order = (lax.axis_index("line") ^ place % line) * 2 + (lax.axis_index("core") ^ place // line)
     tile = pl.pallas_call(

time: 171 us -> 170 us (level)
  blocking collectives: 34.7 us -> 67.8 us
  waiting for transfers between devices: 57.2 us -> 31.2 us
  starting transfers between devices: 46.3 us -> 38.9 us
    all_to_all x0 -> x1, blocking collectives: none -> 33.1 us  [shards(): tiles = lax.all_to_all(tile, 'seq', split_axis=0, concat_axis=0, tiled=True)]
    all_to_all x1 -> x0, waiting for transfers between devices: 18.7 us -> none  [shards(): tiles = lax.all_to_all(tile, 'seq', split_axis=0, concat_axis=0, tiled=True)]
    all_to_all x1 -> x0, starting transfers between devices: 7.33 us -> none  [shards(): tiles = lax.all_to_all(tile, 'seq', split_axis=0, concat_axis=0, tiled=True)]
    all_to_all x1, waiting for transfers between devices: 14.5 us -> 7.21 us  [shards(): lax.all_to_all(columns.reshape(groups, block, enc_rows), ('line', 'core')...]
  transfers between devices with their start and end apart: 8 -> 7, of which waited for: 4 -> 3; matrix products, arithmetic and copies ran while one was open for 6% -> 6% of each run, Pallas kernels for 4% -> 4%
where the time goes in v5:
time: 170 us; the launch traced here: 169 us
  blocking collectives  67.8 us (40%)
  starting transfers between devices  38.9 us (23%)
  waiting for transfers between devices  31.2 us (18%)
  Pallas kernels  15.8 us (9%)
  matrix products  7.27 us (4%)
  local copies, waits for them, and re-layouts  6.87 us (4%)
    all_gather x1, blocking collectives, shards(): lax.all_gather(shared, ('part', 'line', 'core'), axis=0, tiled=True)  34.7 us
    all_to_all x1, blocking collectives, shards(): tiles = lax.all_to_all(tile, 'seq', split_axis=0, concat_axis=0, tiled=True)  33.1 us
    ppermute x3, waiting for transfers between devices, shards(): lax.ppermute(mine, 'line', [(i, i ^ k) for i in range(line)])  20.4 us
    ppermute x3, starting transfers between devices, shards(): lax.ppermute(mine, 'line', [(i, i ^ k) for i in range(line)])  11.7 us
    all_to_all x1, starting transfers between devices, shards(): lax.all_to_all(outgoing.reshape(peers, stride, LANES), 'seq', split_axis=...  10.5 us
    all_to_all x1, starting transfers between devices, shards(): lax.all_to_all(slot_grad.reshape(peers, packed_rows, LANES), 'seq', split...  7.31 us
    dot_general x1, matrix products, contract(): lax.dot_general(a, b, (dims, ((), ())), preferred_element_type=jnp.float32)  7.27 us
    all_to_all x1, waiting for transfers between devices, shards(): lax.all_to_all(columns.reshape(groups, block, enc_rows), ('line', 'core')...  7.21 us
  transfers between devices with their start and end apart: 7, of which 3 were waited for; matrix products, arithmetic and copies ran while one was open for 6% of the time, Pallas kernels for 4%

profile of v5, /device:TPU:1, one launch (start us, length us, event | category | flops | bytes accessed | tf_op | source)
XLA Modules:
  0.0 168.7 jit_solution(4349234183159583664)
XLA Ops:
  0.6 5.7 %shard_map.94 = (bf16[3328,128]{1,0:T(8,128)(2,1)}, bf16[128,192]{1,0:T(8,128)(2,1)}) custom-call(bf16[128,2048]{1,0:T(8,128)(2,1)} %enc_hbm.1, s32[1,128]{1,0:T(1,128)} %bitcast.16, s32[1,128]{1,0:T(1,128)} %bitcast.17, bf16[2048,2048]{1,0:T(8,128)(2,1)} %w_hbm.1), custom_call_target="tpu_custom_call" | custom-call | tf_op jit(solution)/shard_map/pallas_call | solution.py:265
  6.4 10.5 %all-to-all-start = ((bf16[32,104,128]{2,1,0:T(8,128)(2,1)}), bf16[32,104,128]{2,1,0:T(8,128)(2,1)S(1)}, u32[]{:S(2)}, u32[]{:S(2)}) async-start(bf16[32,104,128]{2,1,0:T(8,128)(2,1)} %bitcast.15), calls=%async_computation | async-start | bytes 1703936 | tf_op jit(solution)/shard_map/all_to_all | solution.py:285
  16.9 7.6 %collective-permute-start = (bf16[128,2048]{1,0:T(8,128)(2,1)}, bf16[128,2048]{1,0:T(8,128)(2,1)}, u32[]{:S(2)}, u32[]{:S(2)}) collective-permute-start(bf16[128,2048]{1,0:T(8,128)(2,1)} %enc_hbm.1), channel_id=1, source_target_pairs={{0,192},{64,128},{128,64},{192,0},{1,193},{65,129},{129,65},{193,1... | collective-permute-start | bytes 1572872 | tf_op jit(solution)/shard_map/ppermute | solution.py:284
  24.5 1.9 %collective-permute-start.1 = (bf16[128,2048]{1,0:T(8,128)(2,1)}, bf16[128,2048]{1,0:T(8,128)(2,1)}, u32[]{:S(2)}, u32[]{:S(2)}) collective-permute-start(bf16[128,2048]{1,0:T(8,128)(2,1)} %enc_hbm.1), channel_id=1, source_target_pairs={{0,128},{64,192},{128,0},{192,64},{1,129},{65,193},{129,1},{193,65... | collective-permute-start | bytes 1572872 | tf_op jit(solution)/shard_map/ppermute | solution.py:284
  26.4 2.2 %collective-permute-start.2 = (bf16[128,2048]{1,0:T(8,128)(2,1)}, bf16[128,2048]{1,0:T(8,128)(2,1)}, u32[]{:S(2)}, u32[]{:S(2)}) collective-permute-start(bf16[128,2048]{1,0:T(8,128)(2,1)} %enc_hbm.1), channel_id=1, source_target_pairs={{0,64},{64,0},{128,192},{192,128},{1,65},{65,1},{129,193},{193,129... | collective-permute-start | bytes 1572872 | tf_op jit(solution)/shard_map/ppermute | solution.py:284
  28.6 1.0 copy-done
  29.7 1.0 copy-done.1
  30.7 0.8 copy-done.2
  32.4 3.6 %all-to-all-done = bf16[32,104,128]{2,1,0:T(8,128)(2,1)S(1)} async-done(((bf16[32,104,128]{2,1,0:T(8,128)(2,1)}), bf16[32,104,128]{2,1,0:T(8,128)(2,1)S(1)}, u32[]{:S(2)}, u32[]{:S(2)}) %all-to-all-start) | async-done | bytes 852000 | tf_op jit(solution)/shard_map/all_to_all | solution.py:285
  36.0 4.2 %shard_map.96 = (bf16[256,1024]{1,0:T(8,128)(2,1)}, bf16[3072,128]{1,0:T(8,128)(2,1)}) custom-call(bf16[3328,128]{1,0:T(8,128)(2,1)S(1)} %bitcast.11, s32[1,256]{1,0:T(1,128)S(1)} %get-tuple-element.21.group_ref, bf16[256,1024]{1,0:T(8,128)(2,1)S(1)} %get-tuple-element.22.query_ref, bf16[256,1024]{1,0:T(8,128)(2,1)S(1)} %get-tuple-element.23.grad_ref), custom_call_target="tpu_custom_call" | custom-call | tf_op jit(solution)/shard_map/pallas_call | solution.py:292
  40.2 7.3 %all-to-all-start.1 = ((bf16[32,96,128]{2,1,0:T(8,128)(2,1)}), bf16[32,96,128]{2,1,0:T(8,128)(2,1)S(1)}, u32[]{:S(2)}, u32[]{:S(2)}) async-start(bf16[32,96,128]{2,1,0:T(8,128)(2,1)} %bitcast.5), calls=%async_computation.1 | async-start | bytes 1572864 | tf_op jit(solution)/shard_map/all_to_all | solution.py:308
  47.6 20.4 %collective-permute-done.1 = bf16[128,2048]{1,0:T(8,128)(2,1)} collective-permute-done((bf16[128,2048]{1,0:T(8,128)(2,1)}, bf16[128,2048]{1,0:T(8,128)(2,1)}, u32[]{:S(2)}, u32[]{:S(2)}) %collective-permute-start.1) | collective-permute-done | bytes 524320 | tf_op jit(solution)/shard_map/ppermute | solution.py:284
  68.0 1.1 constant_dynamic-update-slice_fusion.2
  69.1 1.1 constant_dynamic-update-slice_fusion.1
  70.2 1.1 constant_dynamic-update-slice_fusion.own_hbm
  71.3 3.5 %collective-permute-start.3 = (bf16[512,2048]{1,0:T(8,128)(2,1)S(1)}, bf16[512,2048]{1,0:T(8,128)(2,1)}, u32[]{:S(2)}, u32[]{:S(2)}) collective-permute-start(bf16[512,2048]{1,0:T(8,128)(2,1)S(1)} %constant_dynamic-update-slice_fusion.own_hbm), channel_id=1, source_target_pairs={{0,32},{32,0},{1,33},{33,1},{2,34},{34,2},{3,35},{35,3},{4,36},{36... | collective-permute-start | bytes 6291464 | tf_op jit(solution)/shard_map/ppermute | solution.py:307
  74.8 1.7 %shard_map.97 = bf16[2048,128]{1,0:T(8,128)(2,1)} custom-call(bf16[3072,128]{1,0:T(8,128)(2,1)S(1)} %bitcast.13, bf16[128,192]{1,0:T(8,128)(2,1)S(1)} %get-tuple-element.26.placing_ref), custom_call_target="tpu_custom_call" | custom-call | tf_op jit(solution)/shard_map/pallas_call | solution.py:312
  76.4 5.9 %all-to-all-start.2 = ((bf16[8,256,128]{2,1,0:T(8,128)(2,1)}), bf16[8,256,128]{2,1,0:T(8,128)(2,1)S(1)}, u32[]{:S(2)}, u32[]{:S(2)}) async-start(bf16[8,256,128]{2,1,0:T(8,128)(2,1)} %bitcast.7), calls=%async_computation.2 | async-start | bytes 1048576 | tf_op jit(solution)/shard_map/all_to_all | solution.py:320
  82.4 7.3 %convolution_convert_fusion = bf16[128,2048]{1,0:T(8,128)(2,1)} fusion(bf16[2048,128]{1,0:T(8,128)(2,1)} %shard_map.97, bf16[2048,2048]{1,0:T(8,128)(2,1)} %w_hbm.1), kind=kOutput, calls=%fused_computation | convolution fusion | flops 1074003968 | bytes 9437184 | tf_op jit(solution)/shard_map/dot_general | solution.py:20
  89.6 7.2 %all-to-all-done.2.blocks_ref = bf16[8,256,128]{2,1,0:T(8,128)(2,1)S(1)} async-done(((bf16[8,256,128]{2,1,0:T(8,128)(2,1)}), bf16[8,256,128]{2,1,0:T(8,128)(2,1)S(1)}, u32[]{:S(2)}, u32[]{:S(2)}) %all-to-all-start.2) | async-done | bytes 524320 | tf_op jit(solution)/shard_map/all_to_all | solution.py:320
  96.9 2.9 %shard_map.98 = bf16[32,128,128]{2,1,0:T(8,128)(2,1)S(1)} custom-call(s32[8]{0:T(128)S(1)} %fusion.2.order_ref, bf16[8,256,128]{2,1,0:T(8,128)(2,1)S(1)} %all-to-all-done.2.blocks_ref, bf16[512,2048]{1,0:T(8,128)(2,1)S(1)} %constant_dynamic-update-slice_fusion.own_hbm, bf16[512,2048]{1,0:T(8,128)(2,1)} %collective-permute-done.3.other_hbm), custom_call_target="tpu_custom_call" | custom-call | tf_op jit(solution)/shard_map/pallas_call | solution.py:326
  99.8 33.1 %all_to_all.20.parts_ref = bf16[32,128,128]{2,1,0:T(8,128)(2,1)S(1)} all-to-all(bf16[32,128,128]{2,1,0:T(8,128)(2,1)S(1)} %shard_map.98), channel_id=1, replica_groups=mesh['part'=3,'line'=4,'core'=2,'seq'=32] {'seq'}, dimensions={0} | all-to-all | bytes 2097152 | tf_op jit(solution)/shard_map/all_to_all | solution.py:343
  133.1 34.7 %all_gather.3 = bf16[1536,256]{1,0:T(8,128)(2,1)S(1)} all-gather(bf16[64,256]{1,0:T(8,128)(2,1)S(1)} %shard_map.99), channel_id=1, replica_groups=mesh['part'=3,'line'=4,'core'=2,'seq'=32] {'part','line','core'}, dimensions={0}, use_global_device_ids=true | all-gather | bytes 819200 | tf_op jit(solution)/shard_map/all_gather | solution.py:349
  167.8 0.9 shard_map.100
  (15 shorter events, 1.2 us)
Async XLA Ops:
  6.4 29.7 %all-to-all-start = ((bf16[32,104,128]{2,1,0:T(8,128)(2,1)}), bf16[32,104,128]{2,1,0:T(8,128)(2,1)S(1)}, u32[]{:S(2)}, u32[]{:S(2)}) async-start(bf16[32,104,128]{2,1,0:T(8,128)(2,1)} %bitcast.15), calls=%async_computation | async-start | bytes 1703936 | tf_op jit(solution)/shard_map/all_to_all | solution.py:285
  16.9 30.8 %collective-permute-start = (bf16[128,2048]{1,0:T(8,128)(2,1)}, bf16[128,2048]{1,0:T(8,128)(2,1)}, u32[]{:S(2)}, u32[]{:S(2)}) collective-permute-start(bf16[128,2048]{1,0:T(8,128)(2,1)} %enc_hbm.1), channel_id=1, source_target_pairs={{0,192},{64,128},{128,64},{192,0},{1,193},{65,129},{129,65},{193,1... | collective-permute-start | bytes 1572872 | tf_op jit(solution)/shard_map/ppermute | solution.py:284
  24.5 43.5 %collective-permute-start.1 = (bf16[128,2048]{1,0:T(8,128)(2,1)}, bf16[128,2048]{1,0:T(8,128)(2,1)}, u32[]{:S(2)}, u32[]{:S(2)}) collective-permute-start(bf16[128,2048]{1,0:T(8,128)(2,1)} %enc_hbm.1), channel_id=1, source_target_pairs={{0,128},{64,192},{128,0},{192,64},{1,129},{65,193},{129,1},{193,65... | collective-permute-start | bytes 1572872 | tf_op jit(solution)/shard_map/ppermute | solution.py:284
  26.4 41.6 %collective-permute-start.2 = (bf16[128,2048]{1,0:T(8,128)(2,1)}, bf16[128,2048]{1,0:T(8,128)(2,1)}, u32[]{:S(2)}, u32[]{:S(2)}) collective-permute-start(bf16[128,2048]{1,0:T(8,128)(2,1)} %enc_hbm.1), channel_id=1, source_target_pairs={{0,64},{64,0},{128,192},{192,128},{1,65},{65,1},{129,193},{193,129... | collective-permute-start | bytes 1572872 | tf_op jit(solution)/shard_map/ppermute | solution.py:284
  28.6 1.0 copy-start
  29.7 1.0 copy-start.1
  30.7 0.8 copy-start.2
  31.6 0.7 copy-start.3
  32.2 15.3 %copy-start.4 = (bf16[128,2048]{1,0:T(8,128)(2,1)S(1)}, bf16[128,2048]{1,0:T(8,128)(2,1)}, u32[]{:S(2)}) copy-start(bf16[128,2048]{1,0:T(8,128)(2,1)} %enc_hbm.1) | copy-start | bytes 1572868
  40.2 34.5 %all-to-all-start.1 = ((bf16[32,96,128]{2,1,0:T(8,128)(2,1)}), bf16[32,96,128]{2,1,0:T(8,128)(2,1)S(1)}, u32[]{:S(2)}, u32[]{:S(2)}) async-start(bf16[32,96,128]{2,1,0:T(8,128)(2,1)} %bitcast.5), calls=%async_computation.1 | async-start | bytes 1572864 | tf_op jit(solution)/shard_map/all_to_all | solution.py:308
  71.3 25.6 %collective-permute-start.3 = (bf16[512,2048]{1,0:T(8,128)(2,1)S(1)}, bf16[512,2048]{1,0:T(8,128)(2,1)}, u32[]{:S(2)}, u32[]{:S(2)}) collective-permute-start(bf16[512,2048]{1,0:T(8,128)(2,1)S(1)} %constant_dynamic-update-slice_fusion.own_hbm), channel_id=1, source_target_pairs={{0,32},{32,0},{1,33},{33,1},{2,34},{34,2},{3,35},{35,3},{4,36},{36... | collective-permute-start | bytes 6291464 | tf_op jit(solution)/shard_map/ppermute | solution.py:307
  76.4 20.4 %all-to-all-start.2 = ((bf16[8,256,128]{2,1,0:T(8,128)(2,1)}), bf16[8,256,128]{2,1,0:T(8,128)(2,1)S(1)}, u32[]{:S(2)}, u32[]{:S(2)}) async-start(bf16[8,256,128]{2,1,0:T(8,128)(2,1)} %bitcast.7), calls=%async_computation.2 | async-start | bytes 1048576 | tf_op jit(solution)/shard_map/all_to_all | solution.py:320
